TPU v7x, 32 devices: a whole 2x2x4 slice. The times are simulated.
32 devices in a mesh: pipe: 2 (over x), expert: 16 (over z, y, core).
Axes of the slice: x: 2, y: 2, z: 4, core: 2. Of those that a mesh axis runs over, the one named last changes fastest.
Arguments:
- saved_inputs: bfloat16 [2, 3, 1024, 2048], P('pipe', None, 'expert'), may hold values from -6 to 6
- routes: int32 [2, 3, 1024, 4], P('pipe', None, 'expert'), may hold values from 0 to 15, as said below
- gates: float32 [2, 3, 1024, 4], P('pipe', None, 'expert'), may hold values from 0.1 to 0.6
- w_in: bfloat16 [2, 16, 2048, 768], P('pipe', 'expert'), may hold values from -0.125 to 0.125
- w_out: bfloat16 [2, 16, 768, 2048], P('pipe', 'expert'), may hold values from -0.21875 to 0.21875
- cotangent: bfloat16 [3, 1024, 2048], P(None, 'expert', 'pipe'), may hold values from -6 to 6
Outputs:
- grad_in: bfloat16 [3, 1024, 2048], P(None, 'expert', 'pipe')
- grad_w_in: bfloat16 [2, 16, 2048, 768], P('pipe', 'expert')
- grad_w_out: bfloat16 [2, 16, 768, 2048], P('pipe', 'expert')
Inputs may be any that keep to these rules, and one draw needn't show every extreme that they name: `routes`: each token names 4 different experts. Among the 64 tokens of one device's micro-batch (aligned blocks of the token dimension) no expert is named by more than 19 tokens. In every micro-batch of every section some expert is named by exactly 19 tokens in every such block.
All inputs are finite; a program needn't handle non-finite values.
Results may differ from a plain program's by a relative error of at most 0.02.
Values may be sent and summed in bfloat16 or wider, within the bound.
A program may use at most 128 MiB of HBM per device.

v0:
```python
import jax
import jax.numpy as jnp
from jax import lax
from jax.sharding import PartitionSpec as P


def shifted(value, axis, steps):
    count = lax.axis_size(axis)
    first, last = (max(0, -steps), min(count, count - steps))
    return lax.ppermute(value, axis, [(source, source + steps) for source in range(first, last)])


def silu_slope(preactivation):
    logistic = jax.nn.sigmoid(preactivation)
    return logistic * (1.0 + preactivation * (1.0 - logistic))


def placement_tables(routes_micro, expert_count, capacity):
    flat_routes = routes_micro.reshape(-1)
    expert_ids = jnp.arange(expert_count, dtype=jnp.int32)
    one_hot = (flat_routes[:, None] == expert_ids[None, :]).astype(jnp.int32)
    ranks = jnp.sum((jnp.cumsum(one_hot, axis=0) - 1) * one_hot, axis=1)
    slots = flat_routes * capacity + ranks
    slot_ids = jnp.arange(expert_count * capacity, dtype=jnp.int32)
    route_table = (slot_ids[:, None] == slots[None, :]).astype(jnp.bfloat16)
    slot_grid = slots.reshape(routes_micro.shape[0], routes_micro.shape[1])
    token_table = jnp.zeros((expert_count * capacity, routes_micro.shape[0]), jnp.float32)
    for route_no in range(routes_micro.shape[1]):
        token_table = token_table + (slot_ids[:, None] == slot_grid[:, route_no][None, :]).astype(
            jnp.float32
        )
    return (route_table, token_table.astype(jnp.bfloat16))


def on_device(saved_inputs, routes, gates, w_in, w_out, cotangent):
    section_count = lax.axis_size("pipe")
    owners = lax.axis_size("expert")
    section_id = lax.axis_index("pipe")
    micro_count = saved_inputs.shape[1]
    tokens_dev = saved_inputs.shape[2]
    model_width = saved_inputs.shape[3]
    route_count = routes.shape[3]
    local_count = w_in.shape[1]
    expert_count = local_count * owners
    capacity = max(2, tokens_dev * route_count * 6 // (5 * expert_count))
    tick_count = section_count + micro_count - 1
    first_tick = section_count - 1 - section_id
    first_weights = w_in[0, 0]
    second_weights = w_out[0, 0]
    inputs_dev = saved_inputs[0]
    upstream = lax.all_gather(cotangent, "pipe", axis=2, tiled=True)
    pairs = [
        placement_tables(routes[0, micro_no], expert_count, capacity)
        for micro_no in range(micro_count)
    ]
    tables = jnp.stack([pair[0] for pair in pairs])
    token_route_tables = jnp.stack([pair[1] for pair in pairs])
    incoming = jnp.zeros((tokens_dev, model_width), jnp.bfloat16)
    kept_inputs, kept_grads, kept_pre, kept_hidden, kept_out = ([], [], [], [], [])
    for tick_no in range(tick_count):
        micro_id = jnp.clip(tick_no - first_tick, 0, micro_count - 1)
        grad_now = jnp.where(section_id == section_count - 1, upstream[micro_id], incoming)
        gate_now = gates[0, micro_id]
        gate_scaled_rows = (gate_now[:, :, None] * grad_now.astype(jnp.float32)[:, None, :]).astype(
            jnp.bfloat16
        )
        gate_scaled_rows = gate_scaled_rows.reshape(tokens_dev * route_count, model_width)
        gradient_slot_buffer = jnp.dot(
            tables[micro_id], gate_scaled_rows, preferred_element_type=jnp.float32
        ).astype(jnp.bfloat16)
        input_slots = jnp.dot(
            token_route_tables[micro_id], inputs_dev[micro_id], preferred_element_type=jnp.float32
        ).astype(jnp.bfloat16)
        input_recv, grad_recv = (
            lax.all_to_all(input_slots, "expert", split_axis=0, concat_axis=0, tiled=True),
            lax.all_to_all(gradient_slot_buffer, "expert", split_axis=0, concat_axis=0, tiled=True),
        )
        kept_inputs.append(input_recv)
        preactivation = jnp.dot(input_recv, first_weights, preferred_element_type=jnp.float32)
        hidden_grad = lax.dot_general(
            grad_recv, second_weights, (((1,), (1,)), ((), ())), preferred_element_type=jnp.float32
        )
        pre_grad = (hidden_grad * silu_slope(preactivation)).astype(jnp.bfloat16)
        hidden = jax.nn.silu(preactivation).astype(jnp.bfloat16)
        row_grads = lax.dot_general(
            pre_grad, first_weights, (((1,), (1,)), ((), ())), preferred_element_type=jnp.float32
        ).astype(jnp.bfloat16)
        returned = lax.all_to_all(row_grads, "expert", split_axis=0, concat_axis=0, tiled=True)
        summed = lax.dot_general(
            token_route_tables[micro_id],
            returned,
            (((0,), (0,)), ((), ())),
            preferred_element_type=jnp.float32,
        )
        grad_out = (grad_now.astype(jnp.float32) + summed).astype(jnp.bfloat16)
        kept_grads.append(grad_recv)
        kept_pre.append(pre_grad)
        kept_hidden.append(hidden)
        kept_out.append(grad_out)
        if tick_no + 1 < tick_count:
            incoming = shifted(grad_out, "pipe", -1)

    def valid_part(kept):
        return lax.dynamic_slice_in_dim(jnp.stack(kept), first_tick, micro_count, 0)

    gradient_ready_flags = valid_part(kept_grads)
    preactivation_ready = valid_part(kept_pre)
    hidden_ready_flags = valid_part(kept_hidden)
    input_ready_flags = valid_part(kept_inputs)
    first_grad = jnp.einsum(
        "qpz,qpy->zy", input_ready_flags, preactivation_ready, preferred_element_type=jnp.float32
    ).astype(jnp.bfloat16)
    second_grad = jnp.einsum(
        "cgk,cgs->ks", hidden_ready_flags, gradient_ready_flags, preferred_element_type=jnp.float32
    ).astype(jnp.bfloat16)
    final_rows = valid_part(kept_out)
    final_term = jnp.where(section_id == 0, final_rows.astype(jnp.float32), 0.0)
    grad_in = lax.psum_scatter(
        final_term.astype(jnp.bfloat16), "pipe", scatter_dimension=2, tiled=True
    )
    return (grad_in, first_grad[None, None], second_grad[None, None])


def solution(mesh):
    return jax.shard_map(
        on_device,
        mesh=mesh,
        in_specs=(
            P("pipe", None, "expert", None),
            P("pipe", None, "expert", None),
            P("pipe", None, "expert", None),
            P("pipe", "expert", None, None),
            P("pipe", "expert", None, None),
            P(None, "expert", "pipe"),
        ),
        out_specs=(
            P(None, "expert", "pipe"),
            P("pipe", "expert", None, None),
            P("pipe", "expert", None, None),
        ),
        check_vma=False,
    )
```

profile of v0, /device:TPU:16, one launch (start us, length us, event | category | flops | bytes accessed | tf_op | source)
XLA Modules:
  0.0 603.4 jit_solution(14413827804837538923)
XLA Ops:
  13.1 2.5 convolution_convert_fusion.7
  15.5 2.4 all_to_all.99
  17.9 6.2 %all-to-all-start.1 = ((bf16[16,19,2048]{2,1,0:T(8,128)(2,1)}), bf16[16,19,2048]{2,1,0:T(8,128)(2,1)}, u32[]{:S(2)}, u32[]{:S(2)}) async-start(bf16[16,19,2048]{2,1,0:T(8,128)(2,1)} %all_to_all.99), calls=%async_computation.1 | async-start | bytes 3145728 | tf_op jit(solution)/shard_map/all_to_all | solution.py:75
  24.1 12.1 %all_gather.3 = bf16[3,64,2048]{2,1,0:T(8,128)(2,1)S(1)} all-gather(bf16[3,64,1024]{2,1,0:T(8,128)(2,1)} %param.11), channel_id=1, replica_groups=mesh['pipe'=2,'expert'=16] {'pipe'}, dimensions={2}, use_global_device_ids=true | all-gather | bytes 1179648 | tf_op jit(solution)/shard_map/all_gather | solution.py:51
  38.0 2.4 multiply_convert_fusion.3
  43.5 2.8 convolution_convert_fusion.3
  46.3 2.4 all_to_all.96
  48.7 11.9 %all-to-all-done.1 = bf16[16,19,2048]{2,1,0:T(8,128)(2,1)} async-done(((bf16[16,19,2048]{2,1,0:T(8,128)(2,1)}), bf16[16,19,2048]{2,1,0:T(8,128)(2,1)}, u32[]{:S(2)}, u32[]{:S(2)}) %all-to-all-start.1) | async-done | bytes 1245216 | tf_op jit(solution)/shard_map/all_to_all | solution.py:75
  60.6 4.7 all-to-all-start
  67.7 3.4 fusion.22
  71.1 30.7 %all-to-all-done = bf16[16,19,2048]{2,1,0:T(8,128)(2,1)} async-done(((bf16[16,19,2048]{2,1,0:T(8,128)(2,1)}), bf16[16,19,2048]{2,1,0:T(8,128)(2,1)}, u32[]{:S(2)}, u32[]{:S(2)}) %all-to-all-start) | async-done | bytes 1245216 | tf_op jit(solution)/shard_map/all_to_all | solution.py:76
  104.3 3.8 fusion.84
  111.0 2.4 all_to_all.102
  113.4 4.7 all-to-all-start.2
  118.1 2.5 convolution_convert_fusion.6
  120.6 2.4 all_to_all.108
  123.0 31.6 %all-to-all-done.2 = bf16[16,19,2048]{2,1,0:T(8,128)(2,1)} async-done(((bf16[16,19,2048]{2,1,0:T(8,128)(2,1)}), bf16[16,19,2048]{2,1,0:T(8,128)(2,1)}, u32[]{:S(2)}, u32[]{:S(2)}) %all-to-all-start.2) | async-done | bytes 1245216 | tf_op jit(solution)/shard_map/all_to_all | solution.py:88
  154.6 4.7 all-to-all-start.4
  161.7 2.4 fusion.50
  165.6 9.2 %collective-permute-done = bf16[64,2048]{1,0:T(8,128)(2,1)} collective-permute-done((bf16[64,2048]{1,0:T(8,128)(2,1)}, bf16[64,2048]{1,0:T(8,128)(2,1)}, u32[]{:S(2)}, u32[]{:S(2)}) %collective-permute-start) | collective-permute-done | bytes 262176 | tf_op jit(solution)/shard_map/ppermute | solution.py:10
  180.2 2.8 convolution_convert_fusion.2
  183.0 2.4 all_to_all.105
  185.4 10.4 %all-to-all-done.4 = bf16[16,19,2048]{2,1,0:T(8,128)(2,1)} async-done(((bf16[16,19,2048]{2,1,0:T(8,128)(2,1)}), bf16[16,19,2048]{2,1,0:T(8,128)(2,1)}, u32[]{:S(2)}, u32[]{:S(2)}) %all-to-all-start.4) | async-done | bytes 1245216 | tf_op jit(solution)/shard_map/all_to_all | solution.py:75
  195.8 4.7 all-to-all-start.3
  202.9 3.4 fusion.18
  206.3 30.7 %all-to-all-done.3 = bf16[16,19,2048]{2,1,0:T(8,128)(2,1)} async-done(((bf16[16,19,2048]{2,1,0:T(8,128)(2,1)}), bf16[16,19,2048]{2,1,0:T(8,128)(2,1)}, u32[]{:S(2)}, u32[]{:S(2)}) %all-to-all-start.3) | async-done | bytes 1245216 | tf_op jit(solution)/shard_map/all_to_all | solution.py:76
  239.5 3.8 fusion.81
  246.2 2.4 all_to_all.111
  248.6 4.7 all-to-all-start.5
  253.3 2.6 convolution_convert_fusion.5
  258.3 31.5 %all-to-all-done.5 = bf16[16,19,2048]{2,1,0:T(8,128)(2,1)} async-done(((bf16[16,19,2048]{2,1,0:T(8,128)(2,1)}), bf16[16,19,2048]{2,1,0:T(8,128)(2,1)}, u32[]{:S(2)}, u32[]{:S(2)}) %all-to-all-start.5) | async-done | bytes 1245216 | tf_op jit(solution)/shard_map/all_to_all | solution.py:88
  289.8 4.7 all-to-all-start.7
  296.9 2.6 fusion.51
  300.9 9.2 %collective-permute-done.1 = bf16[64,2048]{1,0:T(8,128)(2,1)} collective-permute-done((bf16[64,2048]{1,0:T(8,128)(2,1)}, bf16[64,2048]{1,0:T(8,128)(2,1)}, u32[]{:S(2)}, u32[]{:S(2)}) %collective-permute-start.1) | collective-permute-done | bytes 262176 | tf_op jit(solution)/shard_map/ppermute | solution.py:10
  315.4 2.8 convolution_convert_fusion.1
  318.3 2.4 all_to_all.114
  320.7 10.3 %all-to-all-done.7 = bf16[16,19,2048]{2,1,0:T(8,128)(2,1)} async-done(((bf16[16,19,2048]{2,1,0:T(8,128)(2,1)}), bf16[16,19,2048]{2,1,0:T(8,128)(2,1)}, u32[]{:S(2)}, u32[]{:S(2)}) %all-to-all-start.7) | async-done | bytes 1245216 | tf_op jit(solution)/shard_map/all_to_all | solution.py:75
  331.0 4.7 all-to-all-start.6
  338.1 3.4 fusion.14
  341.5 30.7 %all-to-all-done.6 = bf16[16,19,2048]{2,1,0:T(8,128)(2,1)} async-done(((bf16[16,19,2048]{2,1,0:T(8,128)(2,1)}), bf16[16,19,2048]{2,1,0:T(8,128)(2,1)}, u32[]{:S(2)}, u32[]{:S(2)}) %all-to-all-start.6) | async-done | bytes 1245216 | tf_op jit(solution)/shard_map/all_to_all | solution.py:76
  374.6 3.8 fusion.78
  383.8 4.7 all-to-all-start.8
  388.5 2.5 convolution_convert_fusion.4
  393.4 31.6 %all-to-all-done.8 = bf16[16,19,2048]{2,1,0:T(8,128)(2,1)} async-done(((bf16[16,19,2048]{2,1,0:T(8,128)(2,1)}), bf16[16,19,2048]{2,1,0:T(8,128)(2,1)}, u32[]{:S(2)}, u32[]{:S(2)}) %all-to-all-start.8) | async-done | bytes 1245216 | tf_op jit(solution)/shard_map/all_to_all | solution.py:88
  425.0 17.0 %all-to-all-start.10 = ((bf16[16,19,2048]{2,1,0:T(8,128)(2,1)}), bf16[16,19,2048]{2,1,0:T(8,128)(2,1)}, u32[]{:S(2)}, u32[]{:S(2)}) async-start(bf16[16,19,2048]{2,1,0:T(8,128)(2,1)} %all_to_all.126), calls=%async_computation.10 | async-start | bytes 3145728 | tf_op jit(solution)/shard_map/all_to_all | solution.py:75
  444.5 2.5 fusion.52
  448.4 9.2 %collective-permute-done.2 = bf16[64,2048]{1,0:T(8,128)(2,1)} collective-permute-done((bf16[64,2048]{1,0:T(8,128)(2,1)}, bf16[64,2048]{1,0:T(8,128)(2,1)}, u32[]{:S(2)}, u32[]{:S(2)}) %collective-permute-start.2) | collective-permute-done | bytes 262176 | tf_op jit(solution)/shard_map/ppermute | solution.py:10
  463.0 2.8 convolution_convert_fusion
  465.8 2.4 all_to_all.123
  468.2 10.2 %all-to-all-done.10 = bf16[16,19,2048]{2,1,0:T(8,128)(2,1)} async-done(((bf16[16,19,2048]{2,1,0:T(8,128)(2,1)}), bf16[16,19,2048]{2,1,0:T(8,128)(2,1)}, u32[]{:S(2)}, u32[]{:S(2)}) %all-to-all-start.10) | async-done | bytes 1245216 | tf_op jit(solution)/shard_map/all_to_all | solution.py:75
  478.4 4.7 all-to-all-start.9
  485.5 3.4 fusion.10
  488.9 30.7 %all-to-all-done.9 = bf16[16,19,2048]{2,1,0:T(8,128)(2,1)} async-done(((bf16[16,19,2048]{2,1,0:T(8,128)(2,1)}), bf16[16,19,2048]{2,1,0:T(8,128)(2,1)}, u32[]{:S(2)}, u32[]{:S(2)}) %all-to-all-start.9) | async-done | bytes 1245216 | tf_op jit(solution)/shard_map/all_to_all | solution.py:76
  522.0 3.8 fusion.75
  528.8 2.4 all_to_all.129
  531.2 4.7 all-to-all-start.11
  536.0 2.4 stack.113
  540.8 2.5 stack.100
  543.3 2.5 stack.99
  557.3 2.4 stack.115
  562.2 10.3 %all-to-all-done.11 = bf16[16,19,2048]{2,1,0:T(8,128)(2,1)} async-done(((bf16[16,19,2048]{2,1,0:T(8,128)(2,1)}), bf16[16,19,2048]{2,1,0:T(8,128)(2,1)}, u32[]{:S(2)}, u32[]{:S(2)}) %all-to-all-start.11) | async-done | bytes 1245216 | tf_op jit(solution)/shard_map/all_to_all | solution.py:88
  576.7 2.5 select_convert_fusion
  579.3 8.7 %fusion.35 = bf16[1,1,768,2048]{3,2,1,0:T(8,128)(2,1)} fusion(s32[]{:T(128)S(6)} %select_n.73, bf16[1,304,2048]{2,1,0:T(8,128)(2,1)} %stack.113, bf16[1,304,2048]{2,1,0:T(8,128)(2,1)} %stack.114, bf16[1,304,2048]{2,1,0:T(8,128)(2,1)} %stack.115, bf16[1,304,2048]{2,1,0:T(8,128)(2,1)} %stack.116, bf16[1,304,768]{2,1,0:T(8,128)(2,1)} %fusion.90, ...), kind=kOutput, calls=%fused_computation.41 | convolution fusion | flops 2878181376 | bytes 9995264 | tf_op jit(solution)/shard_map/cgk,cgs->ks/dot_general | solution.py:113
  588.0 7.1 %fusion.32 = bf16[1,1,2048,768]{3,2,1,0:T(8,128)(2,1)} fusion(s32[]{:T(128)S(6)} %select_n.73, bf16[1,304,2048]{2,1,0:T(8,128)(2,1)S(1)} %copy-done.9, bf16[1,304,2048]{2,1,0:T(8,128)(2,1)S(1)} %copy-done.8, bf16[1,304,2048]{2,1,0:T(8,128)(2,1)S(1)} %copy-done.7, bf16[1,304,2048]{2,1,0:T(8,128)(2,1)S(1)} %copy-done.6, ...), kind=kOutput, calls=%fused_computation.40 | convolution fusion | flops 2878181376 | bytes 9995264 | tf_op jit(solution)/shard_map/qpz,qpy->zy/dot_general | solution.py:110
  (139 shorter events, 98.7 us)
Async XLA Ops:
  7.2 60.6 %copy-start = (bf16[1,1,2048,768]{3,2,1,0:T(8,128)(2,1)S(1)}, bf16[1,1,2048,768]{3,2,1,0:T(8,128)(2,1)}, u32[]{:S(2)}) copy-start(bf16[1,1,2048,768]{3,2,1,0:T(8,128)(2,1)} %param.9) | copy-start | bytes 9437188
  17.9 42.7 %all-to-all-start.1 = ((bf16[16,19,2048]{2,1,0:T(8,128)(2,1)}), bf16[16,19,2048]{2,1,0:T(8,128)(2,1)}, u32[]{:S(2)}, u32[]{:S(2)}) async-start(bf16[16,19,2048]{2,1,0:T(8,128)(2,1)} %all_to_all.99), calls=%async_computation.1 | async-start | bytes 3145728 | tf_op jit(solution)/shard_map/all_to_all | solution.py:75
  24.1 13.8 %copy-start.12 = (f32[1,3,64,4]{2,3,1,0:T(4,128)S(1)}, f32[1,3,64,4]{2,3,1,0:T(4,128)}, u32[]{:S(2)}) copy-start(f32[1,3,64,4]{2,3,1,0:T(4,128)} %param.8) | copy-start | bytes 9220
  36.2 0.9 copy-start.1
  42.8 0.7 copy-start.5
  60.6 41.2 %all-to-all-start = ((bf16[16,19,2048]{2,1,0:T(8,128)(2,1)}), bf16[16,19,2048]{2,1,0:T(8,128)(2,1)}, u32[]{:S(2)}, u32[]{:S(2)}) async-start(bf16[16,19,2048]{2,1,0:T(8,128)(2,1)} %all_to_all.96), calls=%async_computation | async-start | bytes 3145728 | tf_op jit(solution)/shard_map/all_to_all | solution.py:76
  108.0 0.8 copy-start.13
  113.4 41.2 %all-to-all-start.2 = ((bf16[16,19,2048]{2,1,0:T(8,128)(2,1)}), bf16[16,19,2048]{2,1,0:T(8,128)(2,1)}, u32[]{:S(2)}, u32[]{:S(2)}) async-start(bf16[16,19,2048]{2,1,0:T(8,128)(2,1)} %all_to_all.102), calls=%async_computation.2 | async-start | bytes 3145728 | tf_op jit(solution)/shard_map/all_to_all | solution.py:88
  154.6 41.2 %all-to-all-start.4 = ((bf16[16,19,2048]{2,1,0:T(8,128)(2,1)}), bf16[16,19,2048]{2,1,0:T(8,128)(2,1)}, u32[]{:S(2)}, u32[]{:S(2)}) async-start(bf16[16,19,2048]{2,1,0:T(8,128)(2,1)} %all_to_all.108), calls=%async_computation.4 | async-start | bytes 3145728 | tf_op jit(solution)/shard_map/all_to_all | solution.py:75
  164.2 10.6 %collective-permute-start = (bf16[64,2048]{1,0:T(8,128)(2,1)}, bf16[64,2048]{1,0:T(8,128)(2,1)}, u32[]{:S(2)}, u32[]{:S(2)}) collective-permute-start(bf16[64,2048]{1,0:T(8,128)(2,1)} %fusion.50), channel_id=1, source_target_pairs={{16,0},{17,1},{18,2},{19,3},{20,4},{21,5},{22,6},{23,7},{24,8},{25... | collective-permute-start | bytes 786440 | tf_op jit(solution)/shard_map/ppermute | solution.py:10
  175.8 0.8 copy-start.3
  195.8 41.2 %all-to-all-start.3 = ((bf16[16,19,2048]{2,1,0:T(8,128)(2,1)}), bf16[16,19,2048]{2,1,0:T(8,128)(2,1)}, u32[]{:S(2)}, u32[]{:S(2)}) async-start(bf16[16,19,2048]{2,1,0:T(8,128)(2,1)} %all_to_all.105), calls=%async_computation.3 | async-start | bytes 3145728 | tf_op jit(solution)/shard_map/all_to_all | solution.py:76
  243.2 0.8 copy-start.15
  248.6 41.2 %all-to-all-start.5 = ((bf16[16,19,2048]{2,1,0:T(8,128)(2,1)}), bf16[16,19,2048]{2,1,0:T(8,128)(2,1)}, u32[]{:S(2)}, u32[]{:S(2)}) async-start(bf16[16,19,2048]{2,1,0:T(8,128)(2,1)} %all_to_all.111), calls=%async_computation.5 | async-start | bytes 3145728 | tf_op jit(solution)/shard_map/all_to_all | solution.py:88
  289.8 41.2 %all-to-all-start.7 = ((bf16[16,19,2048]{2,1,0:T(8,128)(2,1)}), bf16[16,19,2048]{2,1,0:T(8,128)(2,1)}, u32[]{:S(2)}, u32[]{:S(2)}) async-start(bf16[16,19,2048]{2,1,0:T(8,128)(2,1)} %all_to_all.117), calls=%async_computation.7 | async-start | bytes 3145728 | tf_op jit(solution)/shard_map/all_to_all | solution.py:75
  299.5 10.6 %collective-permute-start.1 = (bf16[64,2048]{1,0:T(8,128)(2,1)}, bf16[64,2048]{1,0:T(8,128)(2,1)}, u32[]{:S(2)}, u32[]{:S(2)}) collective-permute-start(bf16[64,2048]{1,0:T(8,128)(2,1)} %fusion.51), channel_id=1, source_target_pairs={{16,0},{17,1},{18,2},{19,3},{20,4},{21,5},{22,6},{23,7},{24,8},{25... | collective-permute-start | bytes 786440 | tf_op jit(solution)/shard_map/ppermute | solution.py:10
  311.1 0.8 copy-start.4
  331.0 41.2 %all-to-all-start.6 = ((bf16[16,19,2048]{2,1,0:T(8,128)(2,1)}), bf16[16,19,2048]{2,1,0:T(8,128)(2,1)}, u32[]{:S(2)}, u32[]{:S(2)}) async-start(bf16[16,19,2048]{2,1,0:T(8,128)(2,1)} %all_to_all.114), calls=%async_computation.6 | async-start | bytes 3145728 | tf_op jit(solution)/shard_map/all_to_all | solution.py:76
  378.4 0.8 copy-start.17
  383.8 41.2 %all-to-all-start.8 = ((bf16[16,19,2048]{2,1,0:T(8,128)(2,1)}), bf16[16,19,2048]{2,1,0:T(8,128)(2,1)}, u32[]{:S(2)}, u32[]{:S(2)}) async-start(bf16[16,19,2048]{2,1,0:T(8,128)(2,1)} %all_to_all.120), calls=%async_computation.8 | async-start | bytes 3145728 | tf_op jit(solution)/shard_map/all_to_all | solution.py:88
  425.0 53.4 %all-to-all-start.10 = ((bf16[16,19,2048]{2,1,0:T(8,128)(2,1)}), bf16[16,19,2048]{2,1,0:T(8,128)(2,1)}, u32[]{:S(2)}, u32[]{:S(2)}) async-start(bf16[16,19,2048]{2,1,0:T(8,128)(2,1)} %all_to_all.126), calls=%async_computation.10 | async-start | bytes 3145728 | tf_op jit(solution)/shard_map/all_to_all | solution.py:75
  447.0 10.6 %collective-permute-start.2 = (bf16[64,2048]{1,0:T(8,128)(2,1)}, bf16[64,2048]{1,0:T(8,128)(2,1)}, u32[]{:S(2)}, u32[]{:S(2)}) collective-permute-start(bf16[64,2048]{1,0:T(8,128)(2,1)} %fusion.52), channel_id=1, source_target_pairs={{16,0},{17,1},{18,2},{19,3},{20,4},{21,5},{22,6},{23,7},{24,8},{25... | collective-permute-start | bytes 786440 | tf_op jit(solution)/shard_map/ppermute | solution.py:10
  458.6 0.8 copy-start.2
  478.4 41.2 %all-to-all-start.9 = ((bf16[16,19,2048]{2,1,0:T(8,128)(2,1)}), bf16[16,19,2048]{2,1,0:T(8,128)(2,1)}, u32[]{:S(2)}, u32[]{:S(2)}) async-start(bf16[16,19,2048]{2,1,0:T(8,128)(2,1)} %all_to_all.123), calls=%async_computation.9 | async-start | bytes 3145728 | tf_op jit(solution)/shard_map/all_to_all | solution.py:76
  525.8 0.8 copy-start.19
  531.2 41.2 %all-to-all-start.11 = ((bf16[16,19,2048]{2,1,0:T(8,128)(2,1)}), bf16[16,19,2048]{2,1,0:T(8,128)(2,1)}, u32[]{:S(2)}, u32[]{:S(2)}) async-start(bf16[16,19,2048]{2,1,0:T(8,128)(2,1)} %all_to_all.129), calls=%async_computation.11 | async-start | bytes 3145728 | tf_op jit(solution)/shard_map/all_to_all | solution.py:88
  535.9 60.5 %reduce-scatter.2.cloned.1.call-start = ((), (), s32[]{:S(2)}) async-start(), calls=%async_computation.13 | async-start | bytes 1179648 | tf_op jit(solution)/shard_map/reduce_scatter | solution.py:118
  548.2 4.6 copy-start.11
  550.5 3.4 copy-start.10
  579.2 8.8 %copy-start.6 = (bf16[1,304,2048]{2,1,0:T(8,128)(2,1)S(1)}, bf16[1,304,2048]{2,1,0:T(8,128)(2,1)}, u32[]{:S(2)}) copy-start(bf16[1,304,2048]{2,1,0:T(8,128)(2,1)} %stack.101) | copy-start | bytes 3735556
  579.2 8.8 %copy-start.7 = (bf16[1,304,2048]{2,1,0:T(8,128)(2,1)S(1)}, bf16[1,304,2048]{2,1,0:T(8,128)(2,1)}, u32[]{:S(2)}) copy-start(bf16[1,304,2048]{2,1,0:T(8,128)(2,1)} %stack.100) | copy-start | bytes 3735556
  579.2 8.8 %copy-start.8 = (bf16[1,304,2048]{2,1,0:T(8,128)(2,1)S(1)}, bf16[1,304,2048]{2,1,0:T(8,128)(2,1)}, u32[]{:S(2)}) copy-start(bf16[1,304,2048]{2,1,0:T(8,128)(2,1)} %stack.99) | copy-start | bytes 3735556
  579.2 8.7 %copy-start.9 = (bf16[1,304,2048]{2,1,0:T(8,128)(2,1)S(1)}, bf16[1,304,2048]{2,1,0:T(8,128)(2,1)}, u32[]{:S(2)}) copy-start(bf16[1,304,2048]{2,1,0:T(8,128)(2,1)} %stack.98) | copy-start | bytes 3735556
  579.2 8.7 %copy-start.14 = (bf16[304,768]{1,0:T(8,128)(2,1)S(1)}, bf16[304,768]{1,0:T(8,128)(2,1)}, u32[]{:S(2)}) copy-start(bf16[304,768]{1,0:T(8,128)(2,1)} %copy-done.13) | copy-start | bytes 1400836
  579.2 8.7 %copy-start.16 = (bf16[304,768]{1,0:T(8,128)(2,1)S(1)}, bf16[304,768]{1,0:T(8,128)(2,1)}, u32[]{:S(2)}) copy-start(bf16[304,768]{1,0:T(8,128)(2,1)} %copy-done.15) | copy-start | bytes 1400836
  579.3 8.7 %copy-start.18 = (bf16[304,768]{1,0:T(8,128)(2,1)S(1)}, bf16[304,768]{1,0:T(8,128)(2,1)}, u32[]{:S(2)}) copy-start(bf16[304,768]{1,0:T(8,128)(2,1)} %copy-done.17) | copy-start | bytes 1400836
  579.3 8.7 %copy-start.20 = (bf16[304,768]{1,0:T(8,128)(2,1)S(1)}, bf16[304,768]{1,0:T(8,128)(2,1)}, u32[]{:S(2)}) copy-start(bf16[304,768]{1,0:T(8,128)(2,1)} %copy-done.19) | copy-start | bytes 1400836
Sparse Core Ops, SparseCore 0:
  579.3 17.0 reduce-scatter.1
where the time goes:
time: 610 us; the launch traced here: 603 us
  waiting for transfers between devices  300 us (49%)
  local copies, waits for them, and re-layouts  97.1 us (16%)
  matrix products  83.6 us (14%)
  starting transfers between devices  73.9 us (12%)
  other arithmetic  22.4 us (4%)
  between operations  14.7 us (2%)
  blocking collectives  12.1 us (2%)
    all_to_all x4, waiting for transfers between devices, on_device(): lax.all_to_all(gradient_slot_buffer, 'expert', split_axis=0, concat_axis=...  123 us
    all_to_all x4, waiting for transfers between devices, on_device(): lax.all_to_all(row_grads, 'expert', split_axis=0, concat_axis=0, tiled=True)  105 us
    all_to_all x4, waiting for transfers between devices, on_device(): lax.all_to_all(input_slots, 'expert', split_axis=0, concat_axis=0, tiled=...  42.9 us
    all_to_all x4, starting transfers between devices, on_device(): lax.all_to_all(input_slots, 'expert', split_axis=0, concat_axis=0, tiled=...  32.6 us
    ppermute x3, waiting for transfers between devices, shifted(): lax.ppermute(value, axis, [(source, source + steps) for source in range(f...  27.5 us
    another operation x8, local copies, waits for them, and re-layouts, valid_part(): return lax.dynamic_slice_in_dim(jnp.stack(kept), first_tick, micro_count, 0)  19.5 us
    all_to_all x8, local copies, waits for them, and re-layouts, on_device(): lax.all_to_all(row_grads, 'expert', split_axis=0, concat_axis=0, tiled=True)  19.4 us
    all_to_all x8, local copies, waits for them, and re-layouts, on_device(): lax.all_to_all(input_slots, 'expert', split_axis=0, concat_axis=0, tiled=...  19.4 us
  transfers between devices with their start and end apart: 16, of which 16 were waited for; matrix products, arithmetic and copies ran while one was open for 17% of the time, Pallas kernels for 0%

commit v1 on v0

v1 whole, which is shorter than its diff:
```python
import jax
import jax.numpy as jnp
from jax import lax
from jax.sharding import PartitionSpec as P


def after(value, earlier):
    nothing = jnp.minimum(jnp.abs(earlier[0, 0].astype(jnp.float32)), 0.0)
    return value + nothing.astype(value.dtype)


def placement(routes_micro, gates_micro, expert_count, capacity):
    tokens, tops = routes_micro.shape
    flat = routes_micro.reshape(-1)
    count = tokens * tops
    one_hot = (flat[:, None] == jnp.arange(expert_count, dtype=jnp.int32)[None, :]).astype(jnp.bfloat16)
    order = jnp.arange(count, dtype=jnp.int32)
    before = (order[:, None] > order[None, :]).astype(jnp.bfloat16)
    earlier = jnp.dot(before, one_hot, preferred_element_type=jnp.float32)
    ranks = jnp.sum(earlier * one_hot.astype(jnp.float32), axis=1).astype(jnp.int32)
    slots = (flat * capacity + ranks).reshape(tokens, tops)
    slot_ids = jnp.arange(expert_count * capacity, dtype=jnp.int32)
    table = jnp.zeros((expert_count * capacity, tokens), jnp.float32)
    slot_gates = jnp.zeros((expert_count * capacity,), jnp.float32)
    for top in range(tops):
        hit = slot_ids[:, None] == slots[:, top][None, :]
        table = table + hit.astype(jnp.float32)
        slot_gates = slot_gates + jnp.sum(jnp.where(hit, gates_micro[:, top][None, :], 0.0), axis=1)
    return table.astype(jnp.bfloat16), slot_gates


def exchange(rows):
    return lax.all_to_all(rows, "expert", split_axis=0, concat_axis=0, tiled=True)


def pick(index, values):
    result = values[-1]
    for number in range(len(values) - 2, -1, -1):
        result = jnp.where(index <= number, values[number], result)
    return result


def on_device(saved_inputs, routes, gates, w_in, w_out, cotangent):
    sections = lax.axis_size("pipe")
    section = lax.axis_index("pipe")
    micros = saved_inputs.shape[1]
    tokens = saved_inputs.shape[2]
    experts = w_in.shape[1] * lax.axis_size("expert")
    capacity = max(2, tokens * routes.shape[3] * 6 // (5 * experts))
    ticks = sections + micros - 1
    first_tick = sections - 1 - section
    last = section == sections - 1
    weight_in, weight_out = w_in[0, 0], w_out[0, 0]
    width = cotangent.shape[2]

    places = [placement(routes[0, m], gates[0, m], experts, capacity) for m in range(micros)]
    tables = [place[0] for place in places]
    slot_gates = [place[1] for place in places]

    def upstream(m):
        own = cotangent[m]
        parts = [
            lax.ppermute(own, "pipe", [(sender, sections - 1)]) for sender in range(sections - 1)
        ]
        return jnp.concatenate(parts + [own], axis=1)

    def send_inputs(m, earlier):
        table = tables[m] if earlier is None else after(tables[m], earlier)
        return exchange(
            jnp.dot(table, saved_inputs[0, m], preferred_element_type=jnp.float32).astype(jnp.bfloat16)
        )

    input_recv, slopes, hiddens = [], [], []

    def take_inputs(received):
        pre = jnp.dot(received, weight_in, preferred_element_type=jnp.float32)
        logistic = jax.nn.sigmoid(pre)
        input_recv.append(received)
        slopes.append(logistic * (1.0 + pre * (1.0 - logistic)))
        hiddens.append((pre * logistic).astype(jnp.bfloat16))

    take_inputs(send_inputs(0, None))
    incoming = None
    grads, pre_grads, outs = [], [], []
    for tick in range(ticks):
        micro = tick - first_tick
        if tick < micros:
            grad_now = upstream(tick)
            if incoming is not None:
                grad_now = jnp.where(last, grad_now, incoming)
        else:
            grad_now = incoming
        table = pick(micro, tables)
        slot_gate = pick(micro, slot_gates)
        if tick == 0:
            table = after(table, input_recv[0])
        placed = jnp.dot(table, grad_now, preferred_element_type=jnp.float32)
        grad_recv = exchange((placed * slot_gate[:, None]).astype(jnp.bfloat16))
        if tick == 0 and micros > 1:
            take_inputs(send_inputs(1, grad_recv))
        hidden_grad = lax.dot_general(
            grad_recv, weight_out, (((1,), (1,)), ((), ())), preferred_element_type=jnp.float32
        )
        known = [slopes[m] for m in range(min(tick + 1, micros))]
        pre_grad = (hidden_grad * pick(micro, known)).astype(jnp.bfloat16)
        row_grads = lax.dot_general(
            pre_grad, weight_in, (((1,), (1,)), ((), ())), preferred_element_type=jnp.float32
        ).astype(jnp.bfloat16)
        returned = exchange(row_grads)
        if tick + 2 < micros:
            take_inputs(send_inputs(tick + 2, returned))
        summed = lax.dot_general(
            table, returned, (((0,), (0,)), ((), ())), preferred_element_type=jnp.float32
        )
        grad_out = (grad_now.astype(jnp.float32) + summed).astype(jnp.bfloat16)
        grads.append(grad_recv)
        pre_grads.append(pre_grad)
        outs.append(grad_out)
        if tick + 1 < ticks:
            incoming = lax.ppermute(
                grad_out, "pipe", [(source, source - 1) for source in range(1, sections)]
            )

    def across(left, right):
        return lax.dot_general(
            left, right, (((0,), (0,)), ((), ())), preferred_element_type=jnp.float32
        )

    grad_in = []
    for m in range(micros):
        rows = outs[sections - 1 + m]
        result = jnp.where(section == 0, rows[:, :width], 0)
        for target in range(1, sections):
            part = rows[:, target * width : (target + 1) * width]
            result = result + lax.ppermute(part, "pipe", [(0, target)])
        grad_in.append(result)

    first, second = 0.0, 0.0
    for m in range(micros):
        mine = pick(first_tick, pre_grads[m : m + sections])
        first = first + across(input_recv[m], mine)
    for tick in range(ticks):
        micro = tick - first_tick
        valid = (micro >= 0) & (micro < micros)
        hidden = jnp.where(valid, pick(micro, hiddens), 0)
        second = second + across(hidden, grads[tick])
    return (
        jnp.stack(grad_in),
        first.astype(jnp.bfloat16)[None, None],
        second.astype(jnp.bfloat16)[None, None],
    )


def solution(mesh):
    return jax.shard_map(
        on_device,
        mesh=mesh,
        in_specs=(
            P("pipe", None, "expert", None),
            P("pipe", None, "expert", None),
            P("pipe", None, "expert", None),
            P("pipe", "expert", None, None),
            P("pipe", "expert", None, None),
            P(None, "expert", "pipe"),
        ),
        out_specs=(
            P(None, "expert", "pipe"),
            P("pipe", "expert", None, None),
            P("pipe", "expert", None, None),
        ),
        check_vma=False,
    )
```

time: 610 us -> 573 us (0.939)
  local copies, waits for them, and re-layouts: 97.1 us -> 66.4 us
  blocking collectives: 12.1 us -> 41.3 us
  waiting for transfers between devices: 300 us -> 271 us
  matrix products: 83.6 us -> 103 us
  other arithmetic: 22.4 us -> 3.92 us
  between operations: 14.7 us -> 4.13 us
    all_to_all x0 -> x1, blocking collectives: none -> 41.3 us  [exchange(): lax.all_to_all(rows, 'expert', split_axis=0, concat_axis=0, tiled=True)]
    all_to_all x12 -> x10, starting transfers between devices: 70 us -> 50.1 us  [exchange(): lax.all_to_all(rows, 'expert', split_axis=0, concat_axis=0, tiled=True)]
    another operation x13 -> x0, local copies, waits for them, and re-layouts: 19.9 us -> none  [the longest x8 19.5 us: valid_part(): return lax.dynamic_slice_in_dim(jnp.stack(kept), first_tick, micro_count, 0)]
    dot_general x26 -> x32, matrix products: 83.6 us -> 103 us  [the longest x7 39.7 us: across(): lax.dot_general(left, right, (((0,), (0,)), ((), ())), preferred_element_...]
    ppermute x3 -> x9, starting transfers between devices: 3.84 us -> 22.9 us  [the longest x3 13.9 us: upstream(): lax.ppermute(own, 'pipe', [(sender, sections - 1)])]
    all_to_all x12 -> x10, waiting for transfers between devices: 271 us -> 255 us  [exchange(): lax.all_to_all(rows, 'expert', split_axis=0, concat_axis=0, tiled=True)]
    convert_element_type x15 -> x3, other arithmetic: 13.4 us -> 0.01 us  [placement(): jnp.sum(earlier * one_hot.astype(jnp.float32), axis=1).astype(jnp.int32)]
    all_gather x1 -> x0, blocking collectives: 12.1 us -> none  [on_device(): upstream = lax.all_gather(cotangent, 'pipe', axis=2, tiled=True)]
  transfers between devices with their start and end apart: 16 -> 19, of which waited for: 16 -> 15; matrix products, arithmetic and copies ran while one was open for 17% -> 15% of each run, Pallas kernels for 0% -> 0%
where the time goes in v1:
time: 573 us; the launch traced here: 563 us
  waiting for transfers between devices  271 us (47%)
  matrix products  103 us (18%)
  starting transfers between devices  72.9 us (13%)
  local copies, waits for them, and re-layouts  66.4 us (12%)
  blocking collectives  41.3 us (7%)
    all_to_all x10, waiting for transfers between devices, exchange(): lax.all_to_all(rows, 'expert', split_axis=0, concat_axis=0, tiled=True)  255 us
    all_to_all x22, local copies, waits for them, and re-layouts, exchange(): lax.all_to_all(rows, 'expert', split_axis=0, concat_axis=0, tiled=True)  53.4 us
    all_to_all x10, starting transfers between devices, exchange(): lax.all_to_all(rows, 'expert', split_axis=0, concat_axis=0, tiled=True)  50.1 us
    all_to_all x1, blocking collectives, exchange(): lax.all_to_all(rows, 'expert', split_axis=0, concat_axis=0, tiled=True)  41.3 us
    dot_general x7, matrix products, across(): lax.dot_general(left, right, (((0,), (0,)), ((), ())), preferred_element_...  39.7 us
    dot_general x4, matrix products, on_device(): lax.dot_general(grad_recv, weight_out, (((1,), (1,)), ((), ())), preferre...  17.9 us
    ppermute x3, starting transfers between devices, upstream(): lax.ppermute(own, 'pipe', [(sender, sections - 1)])  13.9 us
  transfers between devices with their start and end apart: 19, of which 15 were waited for; matrix products, arithmetic and copies ran while one was open for 15% of the time, Pallas kernels for 0%

profile of v1, /device:TPU:16, one launch (start us, length us, event | category | flops | bytes accessed | tf_op | source)
XLA Modules:
  0.0 563.1 jit_solution(15728500998823453324)
XLA Ops:
  2.5 4.0 collective-permute-start.1
  8.0 2.6 convolution_convert_fusion.2
  10.6 2.4 all_to_all.88
  13.1 6.3 %all-to-all-start = ((bf16[16,19,2048]{2,1,0:T(8,128)(2,1)}), bf16[16,19,2048]{2,1,0:T(8,128)(2,1)}, u32[]{:S(2)}, u32[]{:S(2)}) async-start(bf16[16,19,2048]{2,1,0:T(8,128)(2,1)} %all_to_all.88), calls=%async_computation | async-start | bytes 3145728 | tf_op jit(solution)/shard_map/all_to_all | solution.py:33
  23.1 32.8 %all-to-all-done = bf16[16,19,2048]{2,1,0:T(8,128)(2,1)} async-done(((bf16[16,19,2048]{2,1,0:T(8,128)(2,1)}), bf16[16,19,2048]{2,1,0:T(8,128)(2,1)}, u32[]{:S(2)}, u32[]{:S(2)}) %all-to-all-start) | async-done | bytes 1245216 | tf_op jit(solution)/shard_map/all_to_all | solution.py:33
  55.9 2.4 all_to_all.90
  60.2 2.7 fusion.36
  62.8 2.4 all_to_all.91
  65.3 4.7 all-to-all-start.1
  69.9 3.5 multiply_convert_fusion.2
  73.5 33.0 %all-to-all-done.1 = bf16[16,19,2048]{2,1,0:T(8,128)(2,1)} async-done(((bf16[16,19,2048]{2,1,0:T(8,128)(2,1)}), bf16[16,19,2048]{2,1,0:T(8,128)(2,1)}, u32[]{:S(2)}, u32[]{:S(2)}) %all-to-all-start.1) | async-done | bytes 1245216 | tf_op jit(solution)/shard_map/all_to_all | solution.py:33
  106.5 2.5 all_to_all.93
  108.9 3.8 fusion.61
  115.7 2.4 all_to_all.94
  118.1 4.7 all-to-all-start.2
  124.6 2.6 convolution_convert_fusion.1
  127.3 2.4 all_to_all.100
  129.7 29.6 %all-to-all-done.2 = bf16[16,19,2048]{2,1,0:T(8,128)(2,1)} async-done(((bf16[16,19,2048]{2,1,0:T(8,128)(2,1)}), bf16[16,19,2048]{2,1,0:T(8,128)(2,1)}, u32[]{:S(2)}, u32[]{:S(2)}) %all-to-all-start.2) | async-done | bytes 1245216 | tf_op jit(solution)/shard_map/all_to_all | solution.py:33
  159.3 4.7 all-to-all-start.4
  164.0 2.4 all_to_all.96
  166.4 2.5 add_convert_fusion.5
  170.2 5.2 collective-permute-start
  175.5 2.8 collective-permute-done
  179.5 2.7 fusion.37
  182.3 2.4 all_to_all.97
  184.7 15.8 %all-to-all-done.4 = bf16[16,19,2048]{2,1,0:T(8,128)(2,1)} async-done(((bf16[16,19,2048]{2,1,0:T(8,128)(2,1)}), bf16[16,19,2048]{2,1,0:T(8,128)(2,1)}, u32[]{:S(2)}, u32[]{:S(2)}) %all-to-all-start.4) | async-done | bytes 1245216 | tf_op jit(solution)/shard_map/all_to_all | solution.py:33
  200.5 5.0 all-to-all-start.3
  205.5 2.4 all_to_all.102
  207.9 3.6 multiply_convert_fusion.1
  211.5 30.4 %all-to-all-done.3 = bf16[16,19,2048]{2,1,0:T(8,128)(2,1)} async-done(((bf16[16,19,2048]{2,1,0:T(8,128)(2,1)}), bf16[16,19,2048]{2,1,0:T(8,128)(2,1)}, u32[]{:S(2)}, u32[]{:S(2)}) %all-to-all-start.3) | async-done | bytes 1245216 | tf_op jit(solution)/shard_map/all_to_all | solution.py:33
  241.9 2.4 all_to_all.99
  244.3 4.3 fusion.58
  251.6 2.4 all_to_all.103
  254.0 4.7 all-to-all-start.5
  260.6 2.6 convolution_convert_fusion
  263.2 2.4 all_to_all.109
  265.6 29.6 %all-to-all-done.5 = bf16[16,19,2048]{2,1,0:T(8,128)(2,1)} async-done(((bf16[16,19,2048]{2,1,0:T(8,128)(2,1)}), bf16[16,19,2048]{2,1,0:T(8,128)(2,1)}, u32[]{:S(2)}, u32[]{:S(2)}) %all-to-all-start.5) | async-done | bytes 1245216 | tf_op jit(solution)/shard_map/all_to_all | solution.py:33
  295.2 4.7 all-to-all-start.7
  305.7 4.6 collective-permute-start.4
  310.2 2.8 collective-permute-done.4
  317.1 2.4 all_to_all.106
  319.6 16.8 %all-to-all-done.7 = bf16[16,19,2048]{2,1,0:T(8,128)(2,1)} async-done(((bf16[16,19,2048]{2,1,0:T(8,128)(2,1)}), bf16[16,19,2048]{2,1,0:T(8,128)(2,1)}, u32[]{:S(2)}, u32[]{:S(2)}) %all-to-all-start.7) | async-done | bytes 1245216 | tf_op jit(solution)/shard_map/all_to_all | solution.py:33
  336.4 4.7 all-to-all-start.6
  341.1 2.4 all_to_all.111
  343.5 3.6 multiply_convert_fusion
  347.1 30.5 %all-to-all-done.6 = bf16[16,19,2048]{2,1,0:T(8,128)(2,1)} async-done(((bf16[16,19,2048]{2,1,0:T(8,128)(2,1)}), bf16[16,19,2048]{2,1,0:T(8,128)(2,1)}, u32[]{:S(2)}, u32[]{:S(2)}) %all-to-all-start.6) | async-done | bytes 1245216 | tf_op jit(solution)/shard_map/all_to_all | solution.py:33
  380.0 4.9 fusion.55
  387.9 2.4 all_to_all.112
  390.4 41.3 %all_to_all.132 = bf16[16,19,2048]{2,1,0:T(8,128)(2,1)} all-to-all(bf16[16,19,2048]{2,1,0:T(8,128)(2,1)} %all_to_all.112), channel_id=1, replica_groups=mesh['pipe'=2,'expert'=16] {'expert'}, dimensions={0} | all-to-all | bytes 2490368 | tf_op jit(solution)/shard_map/all_to_all | solution.py:33
  438.1 8.2 %collective-permute-done.7 = bf16[64,2048]{1,0:T(8,128)(2,1)S(1)} collective-permute-done((bf16[64,2048]{1,0:T(8,128)(2,1)S(1)}, bf16[64,2048]{1,0:T(8,128)(2,1)S(1)}, u32[]{:S(2)}, u32[]{:S(2)}) %collective-permute-start.7) | collective-permute-done | bytes 262176 | tf_op jit(solution)/shard_map/ppermute | solution.py:120
  448.9 2.4 all_to_all.115
  451.3 5.6 all-to-all-start.9
  456.9 6.2 %fusion.78 = f32[768,2048]{1,0:T(8,128)} fusion(bf16[304,2048]{1,0:T(8,128)(2,1)} %all_to_all.93, bf16[304,768]{1,0:T(8,128)(2,1)} %get-tuple-element.43, bf16[304,768]{1,0:T(8,128)(2,1)} %get-tuple-element.45, bf16[304,768]{1,0:T(8,128)(2,1)} %get-tuple-element.47, pred[]{:T(512)S(6)} %le.19, pred[]{:T(512)S(6)} %le.18, pred[]{:T(512)S(6)} %and.13), kind=kOutput, calls=%fused_computation.79 | convolution fusion | flops 957001728 | bytes 8937475 | tf_op jit(solution)/shard_map/dot_general | solution.py:125
  463.1 4.5 fusion.85
  467.7 4.4 fusion.74
  474.2 19.2 %all-to-all-done.9 = bf16[16,19,2048]{2,1,0:T(8,128)(2,1)} async-done(((bf16[16,19,2048]{2,1,0:T(8,128)(2,1)}), bf16[16,19,2048]{2,1,0:T(8,128)(2,1)}, u32[]{:S(2)}, u32[]{:S(2)}) %all-to-all-start.9) | async-done | bytes 1245216 | tf_op jit(solution)/shard_map/all_to_all | solution.py:33
  495.8 4.9 fusion.52
  503.8 2.4 all_to_all.118
  506.2 5.1 all-to-all-start.10
  512.2 3.4 fusion.70
  517.4 4.5 fusion.83
  522.0 8.5 %fusion.22 = bf16[1,1,768,2048]{3,2,1,0:T(8,128)(2,1)} fusion(bf16[304,2048]{1,0:T(8,128)(2,1)S(1)} %copy-done.10, f32[768,2048]{1,0:T(8,128)S(1)} %fusion.70, f32[768,2048]{1,0:T(8,128)} %fusion.78, f32[768,2048]{1,0:T(8,128)} %fusion.74, bf16[304,768]{1,0:T(8,128)(2,1)S(1)} %copy-done.2, bf16[304,768]{1,0:T(8,128)(2,1)S(1)} %copy-done.4, ...), kind=kOutput, calls=%fused_computation.24 | convolution fusion | flops 963293184 | bytes 24666116 | tf_op jit(solution)/shard_map/dot_general | solution.py:125
  530.5 17.1 %all-to-all-done.10 = bf16[16,19,2048]{2,1,0:T(8,128)(2,1)} async-done(((bf16[16,19,2048]{2,1,0:T(8,128)(2,1)}), bf16[16,19,2048]{2,1,0:T(8,128)(2,1)}, u32[]{:S(2)}, u32[]{:S(2)}) %all-to-all-start.10) | async-done | bytes 1245216 | tf_op jit(solution)/shard_map/all_to_all | solution.py:33
  553.6 8.1 %fusion.23 = bf16[1,1,2048,768]{3,2,1,0:T(8,128)(2,1)} fusion(bf16[304,2048]{1,0:T(8,128)(2,1)S(1)} %copy-done.9, f32[2048,768]{1,0:T(8,128)} %fusion.85, f32[2048,768]{1,0:T(8,128)} %fusion.83, bf16[304,768]{1,0:T(8,128)(2,1)S(1)} %copy-done.17, bf16[304,768]{1,0:T(8,128)(2,1)S(1)} %copy-done.21, pred[]{:T(512)S(6)} %le.26), kind=kOutput, calls=%fused_computation.25 | convolution fusion | flops 961253376 | bytes 17907712 | tf_op jit(solution)/shard_map/dot_general | solution.py:125
  (203 shorter events, 59.8 us)
Async XLA Ops:
  0.6 69.3 %copy-start = (bf16[1,1,2048,768]{3,2,1,0:T(8,128)(2,1)S(1)}, bf16[1,1,2048,768]{3,2,1,0:T(8,128)(2,1)}, u32[]{:S(2)}) copy-start(bf16[1,1,2048,768]{3,2,1,0:T(8,128)(2,1)} %param.9) | copy-start | bytes 9437188
  2.5 177.0 %copy-start.25 = (bf16[64,1024]{1,0:T(8,128)(2,1)}, bf16[64,1024]{1,0:T(8,128)(2,1)S(1)}, u32[]{:S(2)}) copy-start(bf16[64,1024]{1,0:T(8,128)(2,1)S(1)} %get-tuple-element.20) | copy-start | bytes 393220
  2.5 57.7 %collective-permute-start.1 = (bf16[64,1024]{1,0:T(8,128)(2,1)S(1)}, bf16[64,1024]{1,0:T(8,128)(2,1)}, u32[]{:S(2)}, u32[]{:S(2)}) collective-permute-start(bf16[64,1024]{1,0:T(8,128)(2,1)S(1)} %get-tuple-element.21), channel_id=1, source_target_pairs={{0,16},{1,17},{2,18},{3,19},{4,20},{5,21},{6,22},{7,23},{8,24},{9,... | collective-permute-start | bytes 393224 | tf_op jit(solution)/shard_map/ppermute | solution.py:63
  13.1 7.8 %copy-start.26 = (f32[1,3,64,4]{2,3,1,0:T(4,128)S(1)}, f32[1,3,64,4]{2,3,1,0:T(4,128)}, u32[]{:S(2)}) copy-start(f32[1,3,64,4]{2,3,1,0:T(4,128)} %param.8) | copy-start | bytes 9220
  13.1 42.8 %all-to-all-start = ((bf16[16,19,2048]{2,1,0:T(8,128)(2,1)}), bf16[16,19,2048]{2,1,0:T(8,128)(2,1)}, u32[]{:S(2)}, u32[]{:S(2)}) async-start(bf16[16,19,2048]{2,1,0:T(8,128)(2,1)} %all_to_all.88), calls=%async_computation | async-start | bytes 3145728 | tf_op jit(solution)/shard_map/all_to_all | solution.py:33
  20.8 158.7 %copy-start.43 = (s32[64]{0:T(128)}, s32[64]{0:T(128)S(1)}, u32[]{:S(2)}) copy-start(s32[64]{0:T(128)S(1)} %get-tuple-element.57) | copy-start | bytes 772
  20.8 158.7 %copy-start.47 = (s32[64]{0:T(128)}, s32[64]{0:T(128)S(1)}, u32[]{:S(2)}) copy-start(s32[64]{0:T(128)S(1)} %get-tuple-element.58) | copy-start | bytes 772
  20.8 158.7 %copy-start.51 = (s32[64]{0:T(128)}, s32[64]{0:T(128)S(1)}, u32[]{:S(2)}) copy-start(s32[64]{0:T(128)S(1)} %get-tuple-element.59) | copy-start | bytes 772
  20.8 158.7 %copy-start.55 = (s32[64]{0:T(128)}, s32[64]{0:T(128)S(1)}, u32[]{:S(2)}) copy-start(s32[64]{0:T(128)S(1)} %get-tuple-element.60) | copy-start | bytes 772
  20.8 239.7 %copy-start.27 = (s32[64]{0:T(128)}, s32[64]{0:T(128)S(1)}, u32[]{:S(2)}) copy-start(s32[64]{0:T(128)S(1)} %get-tuple-element.3) | copy-start | bytes 772
  20.8 239.7 %copy-start.31 = (s32[64]{0:T(128)}, s32[64]{0:T(128)S(1)}, u32[]{:S(2)}) copy-start(s32[64]{0:T(128)S(1)} %get-tuple-element.4) | copy-start | bytes 772
  20.9 239.7 %copy-start.35 = (s32[64]{0:T(128)}, s32[64]{0:T(128)S(1)}, u32[]{:S(2)}) copy-start(s32[64]{0:T(128)S(1)} %get-tuple-element.5) | copy-start | bytes 772
  20.9 239.7 %copy-start.39 = (s32[64]{0:T(128)}, s32[64]{0:T(128)S(1)}, u32[]{:S(2)}) copy-start(s32[64]{0:T(128)S(1)} %get-tuple-element.6) | copy-start | bytes 772
  65.3 41.2 %all-to-all-start.1 = ((bf16[16,19,2048]{2,1,0:T(8,128)(2,1)}), bf16[16,19,2048]{2,1,0:T(8,128)(2,1)}, u32[]{:S(2)}, u32[]{:S(2)}) async-start(bf16[16,19,2048]{2,1,0:T(8,128)(2,1)} %all_to_all.91), calls=%async_computation.1 | async-start | bytes 3145728 | tf_op jit(solution)/shard_map/all_to_all | solution.py:33
  118.1 41.2 %all-to-all-start.2 = ((bf16[16,19,2048]{2,1,0:T(8,128)(2,1)}), bf16[16,19,2048]{2,1,0:T(8,128)(2,1)}, u32[]{:S(2)}, u32[]{:S(2)}) async-start(bf16[16,19,2048]{2,1,0:T(8,128)(2,1)} %all_to_all.94), calls=%async_computation.2 | async-start | bytes 3145728 | tf_op jit(solution)/shard_map/all_to_all | solution.py:33
  159.3 41.2 %all-to-all-start.4 = ((bf16[16,19,2048]{2,1,0:T(8,128)(2,1)}), bf16[16,19,2048]{2,1,0:T(8,128)(2,1)}, u32[]{:S(2)}, u32[]{:S(2)}) async-start(bf16[16,19,2048]{2,1,0:T(8,128)(2,1)} %all_to_all.100), calls=%async_computation.4 | async-start | bytes 3145728 | tf_op jit(solution)/shard_map/all_to_all | solution.py:33
  168.9 10.6 %collective-permute-start.2 = (bf16[64,2048]{1,0:T(8,128)(2,1)}, bf16[64,2048]{1,0:T(8,128)(2,1)}, u32[]{:S(2)}, u32[]{:S(2)}) collective-permute-start(bf16[64,2048]{1,0:T(8,128)(2,1)} %add_convert_fusion.5), channel_id=1, source_target_pairs={{16,0},{17,1},{18,2},{19,3},{20,4},{21,5},{22,6},{23,7},{24,8},{25... | collective-permute-start | bytes 786440 | tf_op jit(solution)/shard_map/ppermute | solution.py:120
  170.2 8.0 %collective-permute-start = (bf16[64,1024]{1,0:T(8,128)(2,1)S(1)}, bf16[64,1024]{1,0:T(8,128)(2,1)S(1)}, u32[]{:S(2)}, u32[]{:S(2)}) collective-permute-start(bf16[64,1024]{1,0:T(8,128)(2,1)S(1)} %get-tuple-element.20), channel_id=1, source_target_pairs={{0,16},{1,17},{2,18},{3,19},{4,20},{5,21},{6,22},{7,23},{8,24},{9,... | collective-permute-start | bytes 393224 | tf_op jit(solution)/shard_map/ppermute | solution.py:63
  178.3 6.4 %copy-start.63 = (bf16[64,1024]{1,0:T(8,128)(2,1)}, bf16[64,1024]{1,0:T(8,128)(2,1)S(1)}, u32[]{:S(2)}) copy-start(bf16[64,1024]{1,0:T(8,128)(2,1)S(1)} %collective-permute-done) | copy-start | bytes 393220
  200.5 41.4 %all-to-all-start.3 = ((bf16[16,19,2048]{2,1,0:T(8,128)(2,1)}), bf16[16,19,2048]{2,1,0:T(8,128)(2,1)}, u32[]{:S(2)}, u32[]{:S(2)}) async-start(bf16[16,19,2048]{2,1,0:T(8,128)(2,1)} %all_to_all.97), calls=%async_computation.3 | async-start | bytes 3145728 | tf_op jit(solution)/shard_map/all_to_all | solution.py:33
  254.0 41.2 %all-to-all-start.5 = ((bf16[16,19,2048]{2,1,0:T(8,128)(2,1)}), bf16[16,19,2048]{2,1,0:T(8,128)(2,1)}, u32[]{:S(2)}, u32[]{:S(2)}) async-start(bf16[16,19,2048]{2,1,0:T(8,128)(2,1)} %all_to_all.103), calls=%async_computation.5 | async-start | bytes 3145728 | tf_op jit(solution)/shard_map/all_to_all | solution.py:33
  295.2 41.2 %all-to-all-start.7 = ((bf16[16,19,2048]{2,1,0:T(8,128)(2,1)}), bf16[16,19,2048]{2,1,0:T(8,128)(2,1)}, u32[]{:S(2)}, u32[]{:S(2)}) async-start(bf16[16,19,2048]{2,1,0:T(8,128)(2,1)} %all_to_all.109), calls=%async_computation.7 | async-start | bytes 3145728 | tf_op jit(solution)/shard_map/all_to_all | solution.py:33
  302.3 13.0 %copy-start.28 = (s32[64]{0:T(128)S(1)}, s32[64]{0:T(128)}, u32[]{:S(2)}) copy-start(s32[64]{0:T(128)} %copy-done.27) | copy-start | bytes 772
  302.3 13.0 %copy-start.32 = (s32[64]{0:T(128)S(1)}, s32[64]{0:T(128)}, u32[]{:S(2)}) copy-start(s32[64]{0:T(128)} %copy-done.31) | copy-start | bytes 772
  302.3 13.0 %copy-start.36 = (s32[64]{0:T(128)S(1)}, s32[64]{0:T(128)}, u32[]{:S(2)}) copy-start(s32[64]{0:T(128)} %copy-done.35) | copy-start | bytes 772
  302.3 13.0 %copy-start.40 = (s32[64]{0:T(128)S(1)}, s32[64]{0:T(128)}, u32[]{:S(2)}) copy-start(s32[64]{0:T(128)} %copy-done.39) | copy-start | bytes 772
  302.3 13.0 %copy-start.44 = (s32[64]{0:T(128)S(1)}, s32[64]{0:T(128)}, u32[]{:S(2)}) copy-start(s32[64]{0:T(128)} %copy-done.43) | copy-start | bytes 772
  302.3 13.0 %copy-start.48 = (s32[64]{0:T(128)S(1)}, s32[64]{0:T(128)}, u32[]{:S(2)}) copy-start(s32[64]{0:T(128)} %copy-done.47) | copy-start | bytes 772
  302.3 13.0 %copy-start.52 = (s32[64]{0:T(128)S(1)}, s32[64]{0:T(128)}, u32[]{:S(2)}) copy-start(s32[64]{0:T(128)} %copy-done.51) | copy-start | bytes 772
  302.4 13.0 %copy-start.56 = (s32[64]{0:T(128)S(1)}, s32[64]{0:T(128)}, u32[]{:S(2)}) copy-start(s32[64]{0:T(128)} %copy-done.55) | copy-start | bytes 772
  302.4 13.0 %copy-start.60 = (f32[304]{0:T(512)S(1)}, f32[304]{0:T(512)}, u32[]{:S(2)}) copy-start(f32[304]{0:T(512)} %get-tuple-element.22) | copy-start | bytes 3652
  304.3 10.3 %collective-permute-start.5 = (bf16[64,2048]{1,0:T(8,128)(2,1)S(1)}, bf16[64,2048]{1,0:T(8,128)(2,1)S(1)}, u32[]{:S(2)}, u32[]{:S(2)}) collective-permute-start(bf16[64,2048]{1,0:T(8,128)(2,1)S(1)} %add_convert_fusion.4), channel_id=1, source_target_pairs={{16,0},{17,1},{18,2},{19,3},{20,4},{21,5},{22,6},{23,7},{24,8},{25... | collective-permute-start | bytes 786440 | tf_op jit(solution)/shard_map/ppermute | solution.py:120
  305.7 7.3 %collective-permute-start.4 = (bf16[64,1024]{1,0:T(8,128)(2,1)S(1)}, bf16[64,1024]{1,0:T(8,128)(2,1)S(1)}, u32[]{:S(2)}, u32[]{:S(2)}) collective-permute-start(bf16[64,1024]{1,0:T(8,128)(2,1)S(1)} %copy-done.24), channel_id=1, source_target_pairs={{0,16},{1,17},{2,18},{3,19},{4,20},{5,21},{6,22},{7,23},{8,24},{9,... | collective-permute-start | bytes 393224 | tf_op jit(solution)/shard_map/ppermute | solution.py:63
  336.4 41.2 %all-to-all-start.6 = ((bf16[16,19,2048]{2,1,0:T(8,128)(2,1)}), bf16[16,19,2048]{2,1,0:T(8,128)(2,1)}, u32[]{:S(2)}, u32[]{:S(2)}) async-start(bf16[16,19,2048]{2,1,0:T(8,128)(2,1)} %all_to_all.106), calls=%async_computation.6 | async-start | bytes 3145728 | tf_op jit(solution)/shard_map/all_to_all | solution.py:33
  434.1 12.9 %copy-start.29 = (s32[64]{0:T(128)S(1)}, s32[64]{0:T(128)}, u32[]{:S(2)}) copy-start(s32[64]{0:T(128)} %copy-done.27) | copy-start | bytes 772
  434.1 12.9 %copy-start.33 = (s32[64]{0:T(128)S(1)}, s32[64]{0:T(128)}, u32[]{:S(2)}) copy-start(s32[64]{0:T(128)} %copy-done.31) | copy-start | bytes 772
  434.1 12.9 %copy-start.37 = (s32[64]{0:T(128)S(1)}, s32[64]{0:T(128)}, u32[]{:S(2)}) copy-start(s32[64]{0:T(128)} %copy-done.35) | copy-start | bytes 772
  434.1 12.9 %copy-start.41 = (s32[64]{0:T(128)S(1)}, s32[64]{0:T(128)}, u32[]{:S(2)}) copy-start(s32[64]{0:T(128)} %copy-done.39) | copy-start | bytes 772
  434.1 12.9 %copy-start.45 = (s32[64]{0:T(128)S(1)}, s32[64]{0:T(128)}, u32[]{:S(2)}) copy-start(s32[64]{0:T(128)} %copy-done.43) | copy-start | bytes 772
  434.1 12.9 %copy-start.49 = (s32[64]{0:T(128)S(1)}, s32[64]{0:T(128)}, u32[]{:S(2)}) copy-start(s32[64]{0:T(128)} %copy-done.47) | copy-start | bytes 772
  434.1 12.9 %copy-start.53 = (s32[64]{0:T(128)S(1)}, s32[64]{0:T(128)}, u32[]{:S(2)}) copy-start(s32[64]{0:T(128)} %copy-done.51) | copy-start | bytes 772
  434.2 12.9 %copy-start.57 = (s32[64]{0:T(128)S(1)}, s32[64]{0:T(128)}, u32[]{:S(2)}) copy-start(s32[64]{0:T(128)} %copy-done.55) | copy-start | bytes 772
  434.2 12.9 %copy-start.59 = (f32[304]{0:T(512)S(1)}, f32[304]{0:T(512)}, u32[]{:S(2)}) copy-start(f32[304]{0:T(512)} %get-tuple-element.15) | copy-start | bytes 3652
  436.8 9.5 %collective-permute-start.7 = (bf16[64,2048]{1,0:T(8,128)(2,1)S(1)}, bf16[64,2048]{1,0:T(8,128)(2,1)S(1)}, u32[]{:S(2)}, u32[]{:S(2)}) collective-permute-start(bf16[64,2048]{1,0:T(8,128)(2,1)S(1)} %add_convert_fusion.3), channel_id=1, source_target_pairs={{16,0},{17,1},{18,2},{19,3},{20,4},{21,5},{22,6},{23,7},{24,8},{25... | collective-permute-start | bytes 786440 | tf_op jit(solution)/shard_map/ppermute | solution.py:120
  451.3 42.1 %all-to-all-start.9 = ((bf16[16,19,2048]{2,1,0:T(8,128)(2,1)}), bf16[16,19,2048]{2,1,0:T(8,128)(2,1)}, u32[]{:S(2)}, u32[]{:S(2)}) async-start(bf16[16,19,2048]{2,1,0:T(8,128)(2,1)} %all_to_all.115), calls=%async_computation.9 | async-start | bytes 3145728 | tf_op jit(solution)/shard_map/all_to_all | solution.py:33
  456.9 6.2 %copy-start.7 = (bf16[304,2048]{1,0:T(8,128)(2,1)S(1)}, bf16[304,2048]{1,0:T(8,128)(2,1)}, u32[]{:S(2)}) copy-start(bf16[304,2048]{1,0:T(8,128)(2,1)} %all_to_all.90) | copy-start | bytes 3735556
  456.9 6.2 %copy-start.13 = (bf16[304,768]{1,0:T(8,128)(2,1)S(1)}, bf16[304,768]{1,0:T(8,128)(2,1)}, u32[]{:S(2)}) copy-start(bf16[304,768]{1,0:T(8,128)(2,1)} %copy-done.12) | copy-start | bytes 1400836
  456.9 6.2 %copy-start.19 = (bf16[304,768]{1,0:T(8,128)(2,1)S(1)}, bf16[304,768]{1,0:T(8,128)(2,1)}, u32[]{:S(2)}) copy-start(bf16[304,768]{1,0:T(8,128)(2,1)} %copy-done.18) | copy-start | bytes 1400836
  472.1 39.2 %collective-permute-start.3 = (bf16[64,1024]{1,0:T(8,128)(2,1)S(1)}, bf16[64,1024]{1,0:T(8,128)(2,1)}, u32[]{:S(2)}, u32[]{:S(2)}) collective-permute-start(bf16[64,1024]{1,0:T(8,128)(2,1)S(1)} %slice.195), channel_id=1, source_target_pairs={{0,16},{1,17},{2,18},{3,19},{4,20},{5,21},{6,22},{7,23},{8,24},{9,... | collective-permute-start | bytes 393224 | tf_op jit(solution)/shard_map/ppermute | solution.py:135
  506.2 41.4 %all-to-all-start.10 = ((bf16[16,19,2048]{2,1,0:T(8,128)(2,1)}), bf16[16,19,2048]{2,1,0:T(8,128)(2,1)}, u32[]{:S(2)}, u32[]{:S(2)}) async-start(bf16[16,19,2048]{2,1,0:T(8,128)(2,1)} %all_to_all.118), calls=%async_computation.10 | async-start | bytes 3145728 | tf_op jit(solution)/shard_map/all_to_all | solution.py:33
  515.7 6.2 %copy-start.2 = (bf16[304,768]{1,0:T(8,128)(2,1)S(1)}, bf16[304,768]{1,0:T(8,128)(2,1)}, u32[]{:S(2)}) copy-start(bf16[304,768]{1,0:T(8,128)(2,1)} %get-tuple-element.43) | copy-start | bytes 1400836
  515.7 6.2 %copy-start.4 = (bf16[304,768]{1,0:T(8,128)(2,1)S(1)}, bf16[304,768]{1,0:T(8,128)(2,1)}, u32[]{:S(2)}) copy-start(bf16[304,768]{1,0:T(8,128)(2,1)} %get-tuple-element.45) | copy-start | bytes 1400836
  515.7 6.2 %copy-start.6 = (bf16[304,768]{1,0:T(8,128)(2,1)S(1)}, bf16[304,768]{1,0:T(8,128)(2,1)}, u32[]{:S(2)}) copy-start(bf16[304,768]{1,0:T(8,128)(2,1)} %get-tuple-element.47) | copy-start | bytes 1400836
  515.7 6.2 %copy-start.10 = (bf16[304,2048]{1,0:T(8,128)(2,1)S(1)}, bf16[304,2048]{1,0:T(8,128)(2,1)}, u32[]{:S(2)}) copy-start(bf16[304,2048]{1,0:T(8,128)(2,1)} %all_to_all.117) | copy-start | bytes 3735556
  515.8 6.1 %collective-permute-start.6 = (bf16[64,1024]{1,0:T(8,128)(2,1)S(1)}, bf16[64,1024]{1,0:T(8,128)(2,1)S(1)}, u32[]{:S(2)}, u32[]{:S(2)}) collective-permute-start(bf16[64,1024]{1,0:T(8,128)(2,1)S(1)} %slice.198), channel_id=1, source_target_pairs={{0,16},{1,17},{2,18},{3,19},{4,20},{5,21},{6,22},{7,23},{8,24},{9,... | collective-permute-start | bytes 393224 | tf_op jit(solution)/shard_map/ppermute | solution.py:135
  530.5 19.6 %copy-start.30 = (s32[64]{0:T(128)S(1)}, s32[64]{0:T(128)}, u32[]{:S(2)}) copy-start(s32[64]{0:T(128)} %copy-done.27) | copy-start | bytes 772
  530.5 19.6 %copy-start.34 = (s32[64]{0:T(128)S(1)}, s32[64]{0:T(128)}, u32[]{:S(2)}) copy-start(s32[64]{0:T(128)} %copy-done.31) | copy-start | bytes 772
  530.5 19.6 %copy-start.38 = (s32[64]{0:T(128)S(1)}, s32[64]{0:T(128)}, u32[]{:S(2)}) copy-start(s32[64]{0:T(128)} %copy-done.35) | copy-start | bytes 772
  530.5 19.6 %copy-start.42 = (s32[64]{0:T(128)S(1)}, s32[64]{0:T(128)}, u32[]{:S(2)}) copy-start(s32[64]{0:T(128)} %copy-done.39) | copy-start | bytes 772
  530.5 19.6 %copy-start.46 = (s32[64]{0:T(128)S(1)}, s32[64]{0:T(128)}, u32[]{:S(2)}) copy-start(s32[64]{0:T(128)} %copy-done.43) | copy-start | bytes 772
  530.5 19.6 %copy-start.50 = (s32[64]{0:T(128)S(1)}, s32[64]{0:T(128)}, u32[]{:S(2)}) copy-start(s32[64]{0:T(128)} %copy-done.47) | copy-start | bytes 772
  530.5 19.6 %copy-start.54 = (s32[64]{0:T(128)S(1)}, s32[64]{0:T(128)}, u32[]{:S(2)}) copy-start(s32[64]{0:T(128)} %copy-done.51) | copy-start | bytes 772
  530.5 19.6 %copy-start.58 = (s32[64]{0:T(128)S(1)}, s32[64]{0:T(128)}, u32[]{:S(2)}) copy-start(s32[64]{0:T(128)} %copy-done.55) | copy-start | bytes 772
  552.2 9.6 %collective-permute-start.8 = (bf16[64,1024]{1,0:T(8,128)(2,1)S(1)}, bf16[64,1024]{1,0:T(8,128)(2,1)S(1)}, u32[]{:S(2)}, u32[]{:S(2)}) collective-permute-start(bf16[64,1024]{1,0:T(8,128)(2,1)S(1)} %slice.200), channel_id=1, source_target_pairs={{0,16},{1,17},{2,18},{3,19},{4,20},{5,21},{6,22},{7,23},{8,24},{9,... | collective-permute-start | bytes 393224 | tf_op jit(solution)/shard_map/ppermute | solution.py:135
  (20 other events, 57.8 us)

commit v2 on v1

--- a/solution.py
+++ b/solution.py
@@ -1,6 +1,11 @@
+import functools
+import math
+
 import jax
 import jax.numpy as jnp
 from jax import lax
+from jax.experimental import pallas as pl
+from jax.experimental.pallas import tpu as pltpu
 from jax.sharding import PartitionSpec as P
 
 
@@ -9,7 +14,7 @@
     return value + nothing.astype(value.dtype)
 
 
-def placement(routes_micro, gates_micro, expert_count, capacity):
+def placement(routes_micro, expert_count, capacity):
     tokens, tops = routes_micro.shape
     flat = routes_micro.reshape(-1)
     count = tokens * tops
@@ -21,16 +26,172 @@
     slots = (flat * capacity + ranks).reshape(tokens, tops)
     slot_ids = jnp.arange(expert_count * capacity, dtype=jnp.int32)
     table = jnp.zeros((expert_count * capacity, tokens), jnp.float32)
-    slot_gates = jnp.zeros((expert_count * capacity,), jnp.float32)
     for top in range(tops):
         hit = slot_ids[:, None] == slots[:, top][None, :]
         table = table + hit.astype(jnp.float32)
-        slot_gates = slot_gates + jnp.sum(jnp.where(hit, gates_micro[:, top][None, :], 0.0), axis=1)
-    return table.astype(jnp.bfloat16), slot_gates
+    return table.astype(jnp.bfloat16)
 
 
 def exchange(rows):
     return lax.all_to_all(rows, "expert", split_axis=0, concat_axis=0, tiled=True)
+
+
+def gather_kernel(depth, height, arrays, *refs):
+    block_refs, out_refs = refs[:arrays], refs[arrays : 2 * arrays]
+    send_sems, recv_sems, own_sems = refs[2 * arrays :]
+    me = lax.axis_index("expert")
+    core = lax.rem(me, 2)
+    y = lax.rem(me // 2, height)
+    z = me // (2 * height)
+
+    def place(z_at, y_at, core_at):
+        return (z_at * height + y_at) * 2 + core_at
+
+    up, down, right, left, across = range(5)
+    targets = {
+        up: (place(z + 1, y, core), z < depth - 1),
+        down: (place(z - 1, y, core), z > 0),
+        right: (place(z, y + 1, core), y < height - 1),
+        left: (place(z, y - 1, core), y > 0),
+        across: (place(z, y, 1 - core), None),
+    }
+
+    def guarded(condition, action):
+        if condition is None:
+            action()
+        else:
+            pl.when(condition)(action)
+
+    barrier = pltpu.get_barrier_semaphore()
+    for target, exists in targets.values():
+        guarded(
+            exists,
+            functools.partial(
+                pl.semaphore_signal,
+                barrier,
+                inc=1,
+                device_id={"expert": target},
+                device_id_type=pl.DeviceIdType.MESH,
+            ),
+        )
+    owns = [
+        pltpu.make_async_copy(block_refs[k], out_refs[k].at[me], own_sems.at[k]) for k in range(arrays)
+    ]
+    for own in owns:
+        own.start()
+    neighbours = jnp.int32(1)
+    for _, exists in targets.values():
+        if exists is not None:
+            neighbours = neighbours + jnp.where(exists, 1, 0)
+    pl.semaphore_wait(barrier, neighbours)
+
+    sends = []
+
+    def copy(k, way, owner, mine):
+        return pltpu.make_async_remote_copy(
+            src_ref=block_refs[k] if mine else out_refs[k].at[owner],
+            dst_ref=out_refs[k].at[owner],
+            send_sem=send_sems.at[k, way, owner],
+            recv_sem=recv_sems.at[k, owner],
+            device_id={"expert": targets[way][0]},
+            device_id_type=pl.DeviceIdType.MESH,
+        )
+
+    def arrived(owner):
+        for k in range(arrays):
+            copy(k, across, owner, False).wait_recv()
+
+    def forward(owner, ways, present, mine=False):
+        for way in ways:
+            exists = targets[way][1]
+            if present is not None:
+                exists = present if exists is None else present & exists
+            sends.append((way, owner, exists, mine))
+
+            def begin(way=way):
+                for k in range(arrays):
+                    copy(k, way, owner, mine).start()
+
+            guarded(exists, begin)
+
+    forward(me, (up, down, right, left, across), None, True)
+    for step in range(1, depth + height - 1):
+        for y_gap in range(min(step, height - 1) + 1):
+            z_gap = step - y_gap
+            if z_gap > depth - 1:
+                continue
+            for z_sign in (1, -1) if z_gap else (1,):
+                for y_sign in (1, -1) if y_gap else (1,):
+                    z_from, y_from = z - z_sign * z_gap, y - y_sign * y_gap
+                    present = (z_from >= 0) & (z_from < depth) & (y_from >= 0) & (y_from < height)
+                    owner = place(z_from, y_from, core)
+                    pl.when(present)(functools.partial(arrived, owner))
+                    if y_gap:
+                        ways = (right if y_sign > 0 else left, across)
+                    else:
+                        ways = (up if z_sign > 0 else down, right, left, across)
+                    forward(owner, ways, present)
+    for column in range(depth * height):
+        arrived(column * 2 + 1 - core)
+    for way, owner, exists, mine in sends:
+
+        def finish():
+            for k in range(arrays):
+                copy(k, way, owner, mine).wait_send()
+
+        guarded(exists, finish)
+    for own in owns:
+        own.wait()
+
+
+def gather(*blocks):
+    owners = lax.axis_size("expert")
+    height = math.isqrt(owners // 4)
+    depth = owners // (2 * height)
+    arrays = len(blocks)
+    size = sum(block.size * block.dtype.itemsize for block in blocks)
+    return pl.pallas_call(
+        functools.partial(gather_kernel, depth, height, arrays),
+        out_shape=[jax.ShapeDtypeStruct((owners, *block.shape), block.dtype) for block in blocks],
+        in_specs=[pl.BlockSpec(memory_space=pltpu.VMEM)] * arrays,
+        out_specs=[pl.BlockSpec(memory_space=pltpu.VMEM)] * arrays,
+        scratch_shapes=[
+            pltpu.SemaphoreType.DMA((arrays, 5, owners)),
+            pltpu.SemaphoreType.DMA((arrays, owners)),
+            pltpu.SemaphoreType.DMA((arrays,)),
+        ],
+        compiler_params=pltpu.CompilerParams(
+            collective_id=arrays,
+            has_side_effects=True,
+            vmem_limit_bytes=(owners + 2) * size + 2 * 1024 * 1024,
+        ),
+        cost_estimate=pl.CostEstimate(flops=0, bytes_accessed=20 * owners * size, transcendentals=0),
+    )(*blocks)
+
+
+def rows_of(gathered):
+    return gathered.reshape(gathered.shape[0] * gathered.shape[1], gathered.shape[2])
+
+
+def arrivals(routes_all, gates_all, me, capacity):
+    owners, _, tokens = routes_all.shape
+    hit = routes_all == me.astype(jnp.float32)
+    named = jnp.sum(hit.astype(jnp.float32), axis=1)
+    gate = jnp.sum(jnp.where(hit, gates_all, 0.0), axis=1)
+    order = jnp.arange(tokens, dtype=jnp.int32)
+    before = (order[:, None] < order[None, :]).astype(jnp.bfloat16)
+    ranks = jnp.dot(named.astype(jnp.bfloat16), before, preferred_element_type=jnp.float32)
+    starts = jnp.arange(owners, dtype=jnp.int32)[:, None] * capacity
+    slots = jnp.where(named > 0, starts + ranks.astype(jnp.int32), -1).reshape(1, -1)
+    slot_ids = jnp.arange(owners * capacity, dtype=jnp.int32)[:, None]
+    chosen = (slot_ids == slots).astype(jnp.bfloat16)
+    high = lax.reduce_precision(gate, 8, 7)
+    middle = lax.reduce_precision(gate - high, 8, 7)
+    pieces = jnp.stack([high, middle, gate - high - middle]).reshape(3, -1).astype(jnp.bfloat16)
+    split = lax.dot_general(
+        chosen, pieces, (((1,), (1,)), ((), ())), preferred_element_type=jnp.float32
+    )
+    return chosen, split[:, 0] + split[:, 1] + split[:, 2]
 
 
 def pick(index, values):
@@ -53,9 +214,13 @@
     weight_in, weight_out = w_in[0, 0], w_out[0, 0]
     width = cotangent.shape[2]
 
-    places = [placement(routes[0, m], gates[0, m], experts, capacity) for m in range(micros)]
-    tables = [place[0] for place in places]
-    slot_gates = [place[1] for place in places]
+    me = lax.axis_index("expert")
+    tables = [placement(routes[0, m], experts, capacity) for m in range(micros)]
+    tops = routes.shape[3]
+    facts = jnp.concatenate([routes[0].astype(jnp.float32), gates[0]], axis=2).transpose(0, 2, 1)
+    facts = jnp.pad(
+        facts.reshape(micros * 2 * tops, tokens), ((0, 0), (0, -tokens % 128))
+    )
 
     def upstream(m):
         own = cotangent[m]
@@ -64,11 +229,22 @@
         ]
         return jnp.concatenate(parts + [own], axis=1)
 
+    first_block, facts_all = gather(saved_inputs[0, 0], facts)
+    owners = facts_all.shape[0]
+    facts_all = facts_all[:, :, :tokens].reshape(owners, micros, 2 * tops, tokens)
+    taken = [
+        arrivals(facts_all[:, m, :tops], facts_all[:, m, tops:], me, capacity) for m in range(micros)
+    ]
+    take_tables = [part[0] for part in taken]
+    slot_gates = [part[1] for part in taken]
+
+    def take_rows(m, gathered):
+        return jnp.dot(take_tables[m], rows_of(gathered), preferred_element_type=jnp.float32).astype(
+            jnp.bfloat16
+        )
+
     def send_inputs(m, earlier):
-        table = tables[m] if earlier is None else after(tables[m], earlier)
-        return exchange(
-            jnp.dot(table, saved_inputs[0, m], preferred_element_type=jnp.float32).astype(jnp.bfloat16)
-        )
+        return take_rows(m, gather(after(saved_inputs[0, m], earlier))[0])
 
     input_recv, slopes, hiddens = [], [], []
 
@@ -79,7 +255,7 @@
         slopes.append(logistic * (1.0 + pre * (1.0 - logistic)))
         hiddens.append((pre * logistic).astype(jnp.bfloat16))
 
-    take_inputs(send_inputs(0, None))
+    take_inputs(take_rows(0, first_block))
     incoming = None
     grads, pre_grads, outs = [], [], []
     for tick in range(ticks):
@@ -92,10 +268,12 @@
             grad_now = incoming
         table = pick(micro, tables)
         slot_gate = pick(micro, slot_gates)
-        if tick == 0:
-            table = after(table, input_recv[0])
-        placed = jnp.dot(table, grad_now, preferred_element_type=jnp.float32)
-        grad_recv = exchange((placed * slot_gate[:, None]).astype(jnp.bfloat16))
+        placed = jnp.dot(
+            pick(micro, take_tables),
+            rows_of(gather(after(grad_now, first_block[0]) if tick == 0 else grad_now)[0]),
+            preferred_element_type=jnp.float32,
+        )
+        grad_recv = (placed * slot_gate[:, None]).astype(jnp.bfloat16)
         if tick == 0 and micros > 1:
             take_inputs(send_inputs(1, grad_recv))
         hidden_grad = lax.dot_general(

time: 573 us -> 524 us (0.914)
  Pallas kernels: 0 us -> 231 us
  waiting for transfers between devices: 271 us -> 69.8 us
  blocking collectives: 41.3 us -> 0 us
  local copies, waits for them, and re-layouts: 66.4 us -> 48.6 us
  starting transfers between devices: 72.9 us -> 56.6 us
  matrix products: 103 us -> 90 us
  other arithmetic: 3.92 us -> 14.2 us
    pallas_call x0 -> x7, Pallas kernels: none -> 231 us  [gather(): pl.pallas_call(functools.partial(gather_kernel, depth, height, arrays), o...]
    all_to_all x10 -> x4, waiting for transfers between devices: 255 us -> 62.2 us  [exchange(): lax.all_to_all(rows, 'expert', split_axis=0, concat_axis=0, tiled=True)]
    all_to_all x1 -> x0, blocking collectives: 41.3 us -> none  [exchange(): lax.all_to_all(rows, 'expert', split_axis=0, concat_axis=0, tiled=True)]
    all_to_all x22 -> x8, local copies, waits for them, and re-layouts: 53.4 us -> 19.4 us  [exchange(): lax.all_to_all(rows, 'expert', split_axis=0, concat_axis=0, tiled=True)]
    all_to_all x10 -> x4, starting transfers between devices: 50.1 us -> 31.8 us  [exchange(): lax.all_to_all(rows, 'expert', split_axis=0, concat_axis=0, tiled=True)]
    dot_general x4, matrix products: 17.9 us -> 6.67 us  [on_device(): lax.dot_general(grad_recv, weight_out, (((1,), (1,)), ((), ())), preferre...]
    unnamed x133 -> x153, local copies, waits for them, and re-layouts: 5.72 us -> 11.6 us
    dot_general x7 -> x13, matrix products: 16.7 us -> 19.8 us  [the longest x3 7.68 us: take_rows(): jnp.dot(take_tables[m], rows_of(gathered), preferred_element_type=jnp.flo...]
  transfers between devices with their start and end apart: 19 -> 13, of which waited for: 15 -> 4; matrix products, arithmetic and copies ran while one was open for 15% -> 19% of each run, Pallas kernels for 0% -> 28%
where the time goes in v2:
time: 524 us; the launch traced here: 515 us
  Pallas kernels  231 us (44%)
  matrix products  90 us (17%)
  waiting for transfers between devices  69.8 us (13%)
  starting transfers between devices  56.6 us (11%)
  local copies, waits for them, and re-layouts  48.6 us (9%)
  other arithmetic  14.2 us (3%)
    pallas_call x7, Pallas kernels, gather(): pl.pallas_call(functools.partial(gather_kernel, depth, height, arrays), o...  231 us
    all_to_all x4, waiting for transfers between devices, exchange(): lax.all_to_all(rows, 'expert', split_axis=0, concat_axis=0, tiled=True)  62.2 us
    dot_general x7, matrix products, across(): lax.dot_general(left, right, (((0,), (0,)), ((), ())), preferred_element_...  39.9 us
    all_to_all x4, starting transfers between devices, exchange(): lax.all_to_all(rows, 'expert', split_axis=0, concat_axis=0, tiled=True)  31.8 us
    all_to_all x8, local copies, waits for them, and re-layouts, exchange(): lax.all_to_all(rows, 'expert', split_axis=0, concat_axis=0, tiled=True)  19.4 us
    unnamed x153, local copies, waits for them, and re-layouts  11.6 us
    ppermute x3, starting transfers between devices, upstream(): lax.ppermute(own, 'pipe', [(sender, sections - 1)])  11.6 us
  transfers between devices with their start and end apart: 13, of which 4 were waited for; matrix products, arithmetic and copies ran while one was open for 19% of the time, Pallas kernels for 28%

profile of v2, /device:TPU:16, one launch (start us, length us, event | category | flops | bytes accessed | tf_op | source)
XLA Modules:
  0.0 514.6 jit_solution(6475357752570410862)
XLA Ops:
  1.9 4.1 collective-permute-start.1
  8.8 29.7 %shard_map.85 = (bf16[16,64,2048]{2,1,0:T(8,128)(2,1)S(1)}, f32[16,24,128]{2,1,0:T(8,128)S(1)}) custom-call(bf16[64,2048]{1,0:T(8,128)(2,1)S(1)} %slice_bitcast_fusion.1.refs_0_, f32[24,128]{1,0:T(8,128)S(1)} %pad.4.refs_1_), custom_call_target="tpu_custom_call" | custom-call | bytes 87818240 | tf_op jit(solution)/shard_map/pallas_call | solution.py:153
  38.6 1.9 copy-done.2
  41.3 1.4 reduce_sum.98
  49.0 1.7 slice_bitcast_fusion
  52.7 3.6 convolution_convert_fusion.2
  56.4 2.3 multiply_convert_fusion.2
  61.4 1.4 fusion.228
  63.8 29.4 %shard_map.86 = bf16[16,64,2048]{2,1,0:T(8,128)(2,1)S(1)} custom-call(bf16[64,2048]{1,0:T(8,128)(2,1)S(1)} %fusion.160.refs_0_), custom_call_target="tpu_custom_call" | custom-call | bytes 83886080 | tf_op jit(solution)/shard_map/pallas_call | solution.py:153
  93.4 1.6 fusion.24
  95.5 1.3 fusion.61
  97.6 2.2 fusion.28
  99.8 2.4 all_to_all.32
  102.2 9.4 %all-to-all-start = ((bf16[16,19,2048]{2,1,0:T(8,128)(2,1)}), bf16[16,19,2048]{2,1,0:T(8,128)(2,1)}, u32[]{:S(2)}, u32[]{:S(2)}) async-start(bf16[16,19,2048]{2,1,0:T(8,128)(2,1)} %all_to_all.32), calls=%async_computation | async-start | bytes 3145728 | tf_op jit(solution)/shard_map/all_to_all | solution.py:36
  111.6 2.4 collective-permute-start
  114.6 1.4 copy.17
  128.1 20.0 %all-to-all-done = bf16[16,19,2048]{2,1,0:T(8,128)(2,1)} async-done(((bf16[16,19,2048]{2,1,0:T(8,128)(2,1)}), bf16[16,19,2048]{2,1,0:T(8,128)(2,1)}, u32[]{:S(2)}, u32[]{:S(2)}) %all-to-all-start) | async-done | bytes 1245216 | tf_op jit(solution)/shard_map/all_to_all | solution.py:36
  148.1 2.4 all_to_all.34
  152.5 1.9 add_convert_fusion.5
  156.4 28.1 %shard_map.88 = bf16[16,64,2048]{2,1,0:T(8,128)(2,1)S(1)} custom-call(bf16[64,2048]{1,0:T(8,128)(2,1)S(1)} %get-tuple-element.30.refs_0_), custom_call_target="tpu_custom_call" | custom-call | bytes 83886080 | tf_op jit(solution)/shard_map/pallas_call | solution.py:153
  184.5 1.5 convolution_convert_fusion.1
  186.0 2.0 multiply_convert_fusion.1
  189.2 30.9 %shard_map.87 = bf16[16,64,2048]{2,1,0:T(8,128)(2,1)S(1)} custom-call(bf16[64,2048]{1,0:T(8,128)(2,1)S(1)} %maximum_select_fusion.refs_0_), custom_call_target="tpu_custom_call" | custom-call | bytes 83886080 | tf_op jit(solution)/shard_map/pallas_call | solution.py:153
  220.2 1.6 fusion.25
  222.4 1.6 fusion.58
  224.8 2.2 fusion.31
  227.0 2.4 all_to_all.35
  229.4 7.0 %all-to-all-start.1 = ((bf16[16,19,2048]{2,1,0:T(8,128)(2,1)}), bf16[16,19,2048]{2,1,0:T(8,128)(2,1)}, u32[]{:S(2)}, u32[]{:S(2)}) async-start(bf16[16,19,2048]{2,1,0:T(8,128)(2,1)} %all_to_all.35), calls=%async_computation.1 | async-start | bytes 3145728 | tf_op jit(solution)/shard_map/all_to_all | solution.py:36
  236.3 5.2 %collective-permute-start.4 = (bf16[64,1024]{1,0:T(8,128)(2,1)S(1)}, bf16[64,1024]{1,0:T(8,128)(2,1)}, u32[]{:S(2)}, u32[]{:S(2)}) collective-permute-start(bf16[64,1024]{1,0:T(8,128)(2,1)S(1)} %get-tuple-element.31), channel_id=1, source_target_pairs={{0,16},{1,17},{2,18},{3,19},{4,20},{5,21},{6,22},{7,23},{8,24},{9,... | collective-permute-start | bytes 393224 | tf_op jit(solution)/shard_map/ppermute | solution.py:228
  242.5 55.9 %shard_map.90 = bf16[16,64,2048]{2,1,0:T(8,128)(2,1)S(1)} custom-call(bf16[64,2048]{1,0:T(8,128)(2,1)S(1)} %copy-done.1), custom_call_target="tpu_custom_call" | custom-call | bytes 83886080 | tf_op jit(solution)/shard_map/pallas_call | solution.py:153
  298.4 2.5 convolution_convert_fusion
  300.9 2.4 all_to_all.37
  303.3 2.0 add_convert_fusion.4
  306.6 2.0 multiply_convert_fusion
  308.6 7.6 %collective-permute-done.5 = bf16[64,2048]{1,0:T(8,128)(2,1)S(1)} collective-permute-done((bf16[64,2048]{1,0:T(8,128)(2,1)S(1)}, bf16[64,2048]{1,0:T(8,128)(2,1)S(1)}, u32[]{:S(2)}, u32[]{:S(2)}) %collective-permute-start.5) | collective-permute-done | bytes 262176 | tf_op jit(solution)/shard_map/ppermute | solution.py:298
  317.3 28.8 %shard_map.89 = bf16[16,64,2048]{2,1,0:T(8,128)(2,1)S(1)} custom-call(bf16[64,2048]{1,0:T(8,128)(2,1)S(1)} %maximum_select_fusion.1.refs_0_), custom_call_target="tpu_custom_call" | custom-call | bytes 83886080 | tf_op jit(solution)/shard_map/pallas_call | solution.py:153
  346.2 1.6 fusion.26
  348.6 1.9 fusion.55
  351.3 2.2 fusion.34
  353.5 2.4 all_to_all.38
  355.9 7.6 %all-to-all-start.2 = ((bf16[16,19,2048]{2,1,0:T(8,128)(2,1)}), bf16[16,19,2048]{2,1,0:T(8,128)(2,1)}, u32[]{:S(2)}, u32[]{:S(2)}) async-start(bf16[16,19,2048]{2,1,0:T(8,128)(2,1)} %all_to_all.38), calls=%async_computation.2 | async-start | bytes 3145728 | tf_op jit(solution)/shard_map/all_to_all | solution.py:36
  363.6 6.2 %fusion.132 = f32[768,2048]{1,0:T(8,128)} fusion(bf16[304,2048]{1,0:T(8,128)(2,1)} %copy-done.23, bf16[304,768]{1,0:T(8,128)(2,1)} %get-tuple-element.49, bf16[304,768]{1,0:T(8,128)(2,1)} %get-tuple-element.51, bf16[304,768]{1,0:T(8,128)(2,1)} %get-tuple-element.53, pred[]{:T(512)S(6)} %le.19, pred[]{:T(512)S(6)} %le.18, pred[]{:T(512)S(6)} %and.14), kind=kOutput, calls=%fused_computation.131 | convolution fusion | flops 957001728 | bytes 8937475 | tf_op jit(solution)/shard_map/dot_general | solution.py:303
  369.8 4.5 fusion.128
  374.3 25.6 %all-to-all-done.2 = bf16[16,19,2048]{2,1,0:T(8,128)(2,1)} async-done(((bf16[16,19,2048]{2,1,0:T(8,128)(2,1)}), bf16[16,19,2048]{2,1,0:T(8,128)(2,1)}, u32[]{:S(2)}, u32[]{:S(2)}) %all-to-all-start.2) | async-done | bytes 1245216 | tf_op jit(solution)/shard_map/all_to_all | solution.py:36
  399.9 2.4 all_to_all.40
  402.4 2.0 add_convert_fusion.3
  404.4 1.4 collective-permute-start.7
  405.8 4.5 fusion.139
  410.4 6.2 %collective-permute-start.3 = (bf16[64,1024]{1,0:T(8,128)(2,1)S(1)}, bf16[64,1024]{1,0:T(8,128)(2,1)}, u32[]{:S(2)}, u32[]{:S(2)}) collective-permute-start(bf16[64,1024]{1,0:T(8,128)(2,1)S(1)} %slice.218), channel_id=1, source_target_pairs={{0,16},{1,17},{2,18},{3,19},{4,20},{5,21},{6,22},{7,23},{8,24},{9,... | collective-permute-start | bytes 393224 | tf_op jit(solution)/shard_map/ppermute | solution.py:313
  416.6 28.3 %shard_map.91 = bf16[16,64,2048]{2,1,0:T(8,128)(2,1)S(1)} custom-call(bf16[64,2048]{1,0:T(8,128)(2,1)S(1)} %collective-permute-done.7.refs_0_), custom_call_target="tpu_custom_call" | custom-call | bytes 83886080 | tf_op jit(solution)/shard_map/pallas_call | solution.py:153
  445.0 1.6 fusion.27
  447.6 1.9 fusion.52
  450.3 2.2 fusion.37
  452.5 2.4 all_to_all.41
  454.9 7.9 %all-to-all-start.3 = ((bf16[16,19,2048]{2,1,0:T(8,128)(2,1)}), bf16[16,19,2048]{2,1,0:T(8,128)(2,1)}, u32[]{:S(2)}, u32[]{:S(2)}) async-start(bf16[16,19,2048]{2,1,0:T(8,128)(2,1)} %all_to_all.41), calls=%async_computation.3 | async-start | bytes 3145728 | tf_op jit(solution)/shard_map/all_to_all | solution.py:36
  463.8 3.4 fusion.124
  467.3 1.4 collective-permute-start.6
  468.8 4.5 fusion.137
  474.0 8.5 %fusion.22 = bf16[1,1,768,2048]{3,2,1,0:T(8,128)(2,1)} fusion(bf16[304,2048]{1,0:T(8,128)(2,1)S(1)} %copy-done.22, f32[768,2048]{1,0:T(8,128)S(1)} %fusion.124, f32[768,2048]{1,0:T(8,128)} %fusion.132, f32[768,2048]{1,0:T(8,128)} %fusion.128, bf16[304,768]{1,0:T(8,128)(2,1)S(1)} %copy-done.4, bf16[304,768]{1,0:T(8,128)(2,1)S(1)} %copy-done.6, ...), kind=kOutput, calls=%fused_computation.24 | convolution fusion | flops 963293184 | bytes 24666116 | tf_op jit(solution)/shard_map/dot_general | solution.py:303
  482.5 16.6 %all-to-all-done.3 = bf16[16,19,2048]{2,1,0:T(8,128)(2,1)} async-done(((bf16[16,19,2048]{2,1,0:T(8,128)(2,1)}), bf16[16,19,2048]{2,1,0:T(8,128)(2,1)}, u32[]{:S(2)}, u32[]{:S(2)}) %all-to-all-start.3) | async-done | bytes 1245216 | tf_op jit(solution)/shard_map/all_to_all | solution.py:36
  499.1 2.4 all_to_all.43
  501.6 2.0 add_convert_fusion.2
  503.6 1.4 collective-permute-start.8
  505.1 8.3 %fusion.23 = bf16[1,1,2048,768]{3,2,1,0:T(8,128)(2,1)} fusion(bf16[304,2048]{1,0:T(8,128)(2,1)S(1)} %copy-done.20, f32[2048,768]{1,0:T(8,128)} %fusion.139, f32[2048,768]{1,0:T(8,128)} %fusion.137, bf16[304,768]{1,0:T(8,128)(2,1)S(1)} %copy-done.18, bf16[304,768]{1,0:T(8,128)(2,1)} %copy-done.36, pred[]{:T(512)S(6)} %le.26), kind=kOutput, calls=%fused_computation.25 | convolution fusion | flops 961253376 | bytes 17907712 | tf_op jit(solution)/shard_map/dot_general | solution.py:303
  (218 shorter events, 44.3 us)
Async XLA Ops:
  0.6 55.7 %copy-start = (bf16[1,1,2048,768]{3,2,1,0:T(8,128)(2,1)S(1)}, bf16[1,1,2048,768]{3,2,1,0:T(8,128)(2,1)}, u32[]{:S(2)}) copy-start(bf16[1,1,2048,768]{3,2,1,0:T(8,128)(2,1)} %param.9) | copy-start | bytes 9437188
  1.9 109.7 %copy-start.33 = (bf16[64,1024]{1,0:T(8,128)(2,1)}, bf16[64,1024]{1,0:T(8,128)(2,1)S(1)}, u32[]{:S(2)}) copy-start(bf16[64,1024]{1,0:T(8,128)(2,1)S(1)} %get-tuple-element.32) | copy-start | bytes 393220
  1.9 61.0 %collective-permute-start.1 = (bf16[64,1024]{1,0:T(8,128)(2,1)S(1)}, bf16[64,1024]{1,0:T(8,128)(2,1)}, u32[]{:S(2)}, u32[]{:S(2)}) collective-permute-start(bf16[64,1024]{1,0:T(8,128)(2,1)S(1)} %get-tuple-element.33), channel_id=1, source_target_pairs={{0,16},{1,17},{2,18},{3,19},{4,20},{5,21},{6,22},{7,23},{8,24},{9,... | collective-permute-start | bytes 393224 | tf_op jit(solution)/shard_map/ppermute | solution.py:228
  44.4 48.9 %copy-start.46 = (s32[1024]{0:T(1024)}, s32[1024]{0:T(1024)S(1)}, u32[]{:S(2)}) copy-start(s32[1024]{0:T(1024)S(1)} %eq.360) | copy-start | bytes 12292
  63.8 29.5 %copy-start.50 = (s32[1024]{0:T(1024)S(1)}, s32[1024]{0:T(1024)}, u32[]{:S(2)}) copy-start(s32[1024]{0:T(1024)} %eq.365) | copy-start | bytes 12292
  63.8 29.5 %copy-start.54 = (s32[1024]{0:T(1024)S(1)}, s32[1024]{0:T(1024)}, u32[]{:S(2)}) copy-start(s32[1024]{0:T(1024)} %eq.370) | copy-start | bytes 12292
  102.2 11.8 %copy-start.37 = (s32[1,3,64,4]{2,3,1,0:T(4,128)S(1)}, s32[1,3,64,4]{2,3,1,0:T(4,128)}, u32[]{:S(2)}) copy-start(s32[1,3,64,4]{2,3,1,0:T(4,128)} %param.7) | copy-start | bytes 9220
  102.2 45.9 %all-to-all-start = ((bf16[16,19,2048]{2,1,0:T(8,128)(2,1)}), bf16[16,19,2048]{2,1,0:T(8,128)(2,1)}, u32[]{:S(2)}, u32[]{:S(2)}) async-start(bf16[16,19,2048]{2,1,0:T(8,128)(2,1)} %all_to_all.32), calls=%async_computation | async-start | bytes 3145728 | tf_op jit(solution)/shard_map/all_to_all | solution.py:36
  111.6 76.5 %collective-permute-start = (bf16[64,1024]{1,0:T(8,128)(2,1)S(1)}, bf16[64,1024]{1,0:T(8,128)(2,1)}, u32[]{:S(2)}, u32[]{:S(2)}) collective-permute-start(bf16[64,1024]{1,0:T(8,128)(2,1)S(1)} %get-tuple-element.32), channel_id=1, source_target_pairs={{0,16},{1,17},{2,18},{3,19},{4,20},{5,21},{6,22},{7,23},{8,24},{9,... | collective-permute-start | bytes 393224 | tf_op jit(solution)/shard_map/ppermute | solution.py:228
  150.5 5.1 copy-start.31
  154.4 33.7 %collective-permute-start.2 = (bf16[64,2048]{1,0:T(8,128)(2,1)S(1)}, bf16[64,2048]{1,0:T(8,128)(2,1)S(1)}, u32[]{:S(2)}, u32[]{:S(2)}) collective-permute-start(bf16[64,2048]{1,0:T(8,128)(2,1)S(1)} %add_convert_fusion.5), channel_id=1, source_target_pairs={{16,0},{17,1},{18,2},{19,3},{20,4},{21,5},{22,6},{23,7},{24,8},{25... | collective-permute-start | bytes 786440 | tf_op jit(solution)/shard_map/ppermute | solution.py:298
  156.4 28.1 %copy-start.51 = (s32[1024]{0:T(1024)S(1)}, s32[1024]{0:T(1024)}, u32[]{:S(2)}) copy-start(s32[1024]{0:T(1024)} %eq.365) | copy-start | bytes 12292
  188.1 33.9 %copy-start.70 = (f32[304,768]{1,0:T(8,128)}, f32[304,768]{1,0:T(8,128)S(1)}, u32[]{:S(2)}) copy-start(f32[304,768]{1,0:T(8,128)S(1)} %get-tuple-element.52) | copy-start | bytes 2801668
  189.2 31.0 %copy-start.47 = (s32[1024]{0:T(1024)S(1)}, s32[1024]{0:T(1024)}, u32[]{:S(2)}) copy-start(s32[1024]{0:T(1024)} %copy-done.46) | copy-start | bytes 12292
  189.2 31.0 %copy-start.55 = (s32[1024]{0:T(1024)S(1)}, s32[1024]{0:T(1024)}, u32[]{:S(2)}) copy-start(s32[1024]{0:T(1024)} %eq.370) | copy-start | bytes 12292
  189.2 31.0 %copy-start.61 = (f32[304]{0:T(512)S(1)}, f32[304]{0:T(512)}, u32[]{:S(2)}) copy-start(f32[304]{0:T(512)} %get-tuple-element.27) | copy-start | bytes 3652
  229.4 71.5 %all-to-all-start.1 = ((bf16[16,19,2048]{2,1,0:T(8,128)(2,1)}), bf16[16,19,2048]{2,1,0:T(8,128)(2,1)}, u32[]{:S(2)}, u32[]{:S(2)}) async-start(bf16[16,19,2048]{2,1,0:T(8,128)(2,1)} %all_to_all.35), calls=%async_computation.1 | async-start | bytes 3145728 | tf_op jit(solution)/shard_map/all_to_all | solution.py:36
  236.3 72.3 %collective-permute-start.4 = (bf16[64,1024]{1,0:T(8,128)(2,1)S(1)}, bf16[64,1024]{1,0:T(8,128)(2,1)}, u32[]{:S(2)}, u32[]{:S(2)}) collective-permute-start(bf16[64,1024]{1,0:T(8,128)(2,1)S(1)} %get-tuple-element.31), channel_id=1, source_target_pairs={{0,16},{1,17},{2,18},{3,19},{4,20},{5,21},{6,22},{7,23},{8,24},{9,... | collective-permute-start | bytes 393224 | tf_op jit(solution)/shard_map/ppermute | solution.py:228
  242.5 55.9 %copy-start.56 = (s32[1024]{0:T(1024)S(1)}, s32[1024]{0:T(1024)}, u32[]{:S(2)}) copy-start(s32[1024]{0:T(1024)} %eq.370) | copy-start | bytes 12292
  303.3 3.3 copy-start.19
  305.3 3.3 copy-start.27
  305.3 10.9 %collective-permute-start.5 = (bf16[64,2048]{1,0:T(8,128)(2,1)S(1)}, bf16[64,2048]{1,0:T(8,128)(2,1)S(1)}, u32[]{:S(2)}, u32[]{:S(2)}) collective-permute-start(bf16[64,2048]{1,0:T(8,128)(2,1)S(1)} %add_convert_fusion.4), channel_id=1, source_target_pairs={{16,0},{17,1},{18,2},{19,3},{20,4},{21,5},{22,6},{23,7},{24,8},{25... | collective-permute-start | bytes 786440 | tf_op jit(solution)/shard_map/ppermute | solution.py:298
  308.6 39.2 %copy-start.73 = (f32[304,768]{1,0:T(8,128)}, f32[304,768]{1,0:T(8,128)S(1)}, u32[]{:S(2)}) copy-start(f32[304,768]{1,0:T(8,128)S(1)} %get-tuple-element.54) | copy-start | bytes 2801668
  317.2 28.9 %copy-start.48 = (s32[1024]{0:T(1024)S(1)}, s32[1024]{0:T(1024)}, u32[]{:S(2)}) copy-start(s32[1024]{0:T(1024)} %copy-done.46) | copy-start | bytes 12292
  317.3 28.9 %copy-start.52 = (s32[1024]{0:T(1024)S(1)}, s32[1024]{0:T(1024)}, u32[]{:S(2)}) copy-start(s32[1024]{0:T(1024)} %eq.365) | copy-start | bytes 12292
  317.3 28.9 %copy-start.57 = (s32[1024]{0:T(1024)S(1)}, s32[1024]{0:T(1024)}, u32[]{:S(2)}) copy-start(s32[1024]{0:T(1024)} %eq.370) | copy-start | bytes 12292
  317.3 28.9 %copy-start.60 = (f32[304]{0:T(512)S(1)}, f32[304]{0:T(512)}, u32[]{:S(2)}) copy-start(f32[304]{0:T(512)} %get-tuple-element.26) | copy-start | bytes 3652
  355.9 44.0 %all-to-all-start.2 = ((bf16[16,19,2048]{2,1,0:T(8,128)(2,1)}), bf16[16,19,2048]{2,1,0:T(8,128)(2,1)}, u32[]{:S(2)}, u32[]{:S(2)}) async-start(bf16[16,19,2048]{2,1,0:T(8,128)(2,1)} %all_to_all.38), calls=%async_computation.2 | async-start | bytes 3145728 | tf_op jit(solution)/shard_map/all_to_all | solution.py:36
  363.5 6.2 %copy-start.3 = (bf16[304,768]{1,0:T(8,128)(2,1)S(1)}, bf16[304,768]{1,0:T(8,128)(2,1)}, u32[]{:S(2)}) copy-start(bf16[304,768]{1,0:T(8,128)(2,1)} %get-tuple-element.49) | copy-start | bytes 1400836
  363.5 6.2 %copy-start.5 = (bf16[304,768]{1,0:T(8,128)(2,1)S(1)}, bf16[304,768]{1,0:T(8,128)(2,1)}, u32[]{:S(2)}) copy-start(bf16[304,768]{1,0:T(8,128)(2,1)} %get-tuple-element.51) | copy-start | bytes 1400836
  363.5 6.2 %copy-start.7 = (bf16[304,768]{1,0:T(8,128)(2,1)S(1)}, bf16[304,768]{1,0:T(8,128)(2,1)}, u32[]{:S(2)}) copy-start(bf16[304,768]{1,0:T(8,128)(2,1)} %get-tuple-element.53) | copy-start | bytes 1400836
  363.6 6.2 %copy-start.26 = (bf16[304,2048]{1,0:T(8,128)(2,1)S(1)}, bf16[304,2048]{1,0:T(8,128)(2,1)}, u32[]{:S(2)}) copy-start(bf16[304,2048]{1,0:T(8,128)(2,1)} %copy-done.25) | copy-start | bytes 3735556
  374.3 28.0 %copy-start.38 = (s32[64]{0:T(128)S(1)}, s32[64]{0:T(128)}, u32[]{:S(2)}) copy-start(s32[64]{0:T(128)} %get-tuple-element.10) | copy-start | bytes 772
  374.3 28.0 %copy-start.39 = (s32[64]{0:T(128)S(1)}, s32[64]{0:T(128)}, u32[]{:S(2)}) copy-start(s32[64]{0:T(128)} %get-tuple-element.11) | copy-start | bytes 772
  374.3 28.0 %copy-start.40 = (s32[64]{0:T(128)S(1)}, s32[64]{0:T(128)}, u32[]{:S(2)}) copy-start(s32[64]{0:T(128)} %get-tuple-element.12) | copy-start | bytes 772
  374.3 28.0 %copy-start.41 = (s32[64]{0:T(128)S(1)}, s32[64]{0:T(128)}, u32[]{:S(2)}) copy-start(s32[64]{0:T(128)} %get-tuple-element.13) | copy-start | bytes 772
  374.3 28.0 %copy-start.42 = (s32[64]{0:T(128)S(1)}, s32[64]{0:T(128)}, u32[]{:S(2)}) copy-start(s32[64]{0:T(128)} %get-tuple-element.57) | copy-start | bytes 772
  374.3 28.0 %copy-start.43 = (s32[64]{0:T(128)S(1)}, s32[64]{0:T(128)}, u32[]{:S(2)}) copy-start(s32[64]{0:T(128)} %get-tuple-element.58) | copy-start | bytes 772
  374.3 28.0 %copy-start.44 = (s32[64]{0:T(128)S(1)}, s32[64]{0:T(128)}, u32[]{:S(2)}) copy-start(s32[64]{0:T(128)} %get-tuple-element.59) | copy-start | bytes 772
  374.3 28.0 %copy-start.45 = (s32[64]{0:T(128)S(1)}, s32[64]{0:T(128)}, u32[]{:S(2)}) copy-start(s32[64]{0:T(128)} %get-tuple-element.60) | copy-start | bytes 772
  402.3 3.5 copy-start.10
  402.3 3.5 copy-start.14
  404.3 6.0 %copy-start.29 = (bf16[64,2048]{1,0:T(8,128)(2,1)}, bf16[64,2048]{1,0:T(8,128)(2,1)S(1)}, u32[]{:S(2)}) copy-start(bf16[64,2048]{1,0:T(8,128)(2,1)S(1)} %add_convert_fusion.3) | copy-start | bytes 786436
  404.4 6.0 %copy-start.28 = (bf16[64,2048]{1,0:T(8,128)(2,1)S(1)}, bf16[64,2048]{1,0:T(8,128)(2,1)}, u32[]{:S(2)}) copy-start(bf16[64,2048]{1,0:T(8,128)(2,1)} %copy-done.27) | copy-start | bytes 786436
  404.4 12.2 %collective-permute-start.7 = (bf16[64,2048]{1,0:T(8,128)(2,1)S(1)}, bf16[64,2048]{1,0:T(8,128)(2,1)S(1)}, u32[]{:S(2)}, u32[]{:S(2)}) collective-permute-start(bf16[64,2048]{1,0:T(8,128)(2,1)S(1)} %add_convert_fusion.3), channel_id=1, source_target_pairs={{16,0},{17,1},{18,2},{19,3},{20,4},{21,5},{22,6},{23,7},{24,8},{25... | collective-permute-start | bytes 786440 | tf_op jit(solution)/shard_map/ppermute | solution.py:298
  410.3 34.6 %copy-start.49 = (s32[1024]{0:T(1024)S(1)}, s32[1024]{0:T(1024)}, u32[]{:S(2)}) copy-start(s32[1024]{0:T(1024)} %copy-done.46) | copy-start | bytes 12292
  410.3 34.6 %copy-start.53 = (s32[1024]{0:T(1024)S(1)}, s32[1024]{0:T(1024)}, u32[]{:S(2)}) copy-start(s32[1024]{0:T(1024)} %eq.365) | copy-start | bytes 12292
  410.3 34.6 %copy-start.58 = (s32[1024]{0:T(1024)S(1)}, s32[1024]{0:T(1024)}, u32[]{:S(2)}) copy-start(s32[1024]{0:T(1024)} %eq.370) | copy-start | bytes 12292
  410.4 34.6 %copy-start.59 = (f32[304]{0:T(512)S(1)}, f32[304]{0:T(512)}, u32[]{:S(2)}) copy-start(f32[304]{0:T(512)} %get-tuple-element.25) | copy-start | bytes 3652
  410.4 52.4 %collective-permute-start.3 = (bf16[64,1024]{1,0:T(8,128)(2,1)S(1)}, bf16[64,1024]{1,0:T(8,128)(2,1)}, u32[]{:S(2)}, u32[]{:S(2)}) collective-permute-start(bf16[64,1024]{1,0:T(8,128)(2,1)S(1)} %slice.218), channel_id=1, source_target_pairs={{0,16},{1,17},{2,18},{3,19},{4,20},{5,21},{6,22},{7,23},{8,24},{9,... | collective-permute-start | bytes 393224 | tf_op jit(solution)/shard_map/ppermute | solution.py:313
  454.9 44.2 %all-to-all-start.3 = ((bf16[16,19,2048]{2,1,0:T(8,128)(2,1)}), bf16[16,19,2048]{2,1,0:T(8,128)(2,1)}, u32[]{:S(2)}, u32[]{:S(2)}) async-start(bf16[16,19,2048]{2,1,0:T(8,128)(2,1)} %all_to_all.41), calls=%async_computation.3 | async-start | bytes 3145728 | tf_op jit(solution)/shard_map/all_to_all | solution.py:36
  463.8 3.5 copy-start.30
  463.8 5.0 copy-start.12
  463.8 5.0 copy-start.15
  463.8 5.0 copy-start.17
  467.3 6.7 %copy-start.4 = (bf16[304,768]{1,0:T(8,128)(2,1)S(1)}, bf16[304,768]{1,0:T(8,128)(2,1)}, u32[]{:S(2)}) copy-start(bf16[304,768]{1,0:T(8,128)(2,1)} %get-tuple-element.49) | copy-start | bytes 1400836
  467.3 6.7 %copy-start.6 = (bf16[304,768]{1,0:T(8,128)(2,1)S(1)}, bf16[304,768]{1,0:T(8,128)(2,1)}, u32[]{:S(2)}) copy-start(bf16[304,768]{1,0:T(8,128)(2,1)} %get-tuple-element.51) | copy-start | bytes 1400836
  467.3 6.7 %copy-start.8 = (bf16[304,768]{1,0:T(8,128)(2,1)S(1)}, bf16[304,768]{1,0:T(8,128)(2,1)}, u32[]{:S(2)}) copy-start(bf16[304,768]{1,0:T(8,128)(2,1)} %get-tuple-element.53) | copy-start | bytes 1400836
  467.3 6.7 %copy-start.22 = (bf16[304,2048]{1,0:T(8,128)(2,1)S(1)}, bf16[304,2048]{1,0:T(8,128)(2,1)}, u32[]{:S(2)}) copy-start(bf16[304,2048]{1,0:T(8,128)(2,1)} %copy-done.21) | copy-start | bytes 3735556
  467.3 6.0 %collective-permute-start.6 = (bf16[64,1024]{1,0:T(8,128)(2,1)S(1)}, bf16[64,1024]{1,0:T(8,128)(2,1)S(1)}, u32[]{:S(2)}, u32[]{:S(2)}) collective-permute-start(bf16[64,1024]{1,0:T(8,128)(2,1)S(1)} %slice.221), channel_id=1, source_target_pairs={{0,16},{1,17},{2,18},{3,19},{4,20},{5,21},{6,22},{7,23},{8,24},{9,... | collective-permute-start | bytes 393224 | tf_op jit(solution)/shard_map/ppermute | solution.py:313
  501.6 3.5 copy-start.18
  501.6 3.5 copy-start.20
  503.6 9.8 %copy-start.32 = (bf16[1,64,1024]{2,1,0:T(8,128)(2,1)S(1)}, bf16[1,64,1024]{2,1,0:T(8,128)(2,1)}, u32[]{:S(2)}) copy-start(bf16[1,64,1024]{2,1,0:T(8,128)(2,1)} %fusion.164) | copy-start | bytes 393220
  503.6 9.7 %collective-permute-start.8 = (bf16[64,1024]{1,0:T(8,128)(2,1)S(1)}, bf16[64,1024]{1,0:T(8,128)(2,1)S(1)}, u32[]{:S(2)}, u32[]{:S(2)}) collective-permute-start(bf16[64,1024]{1,0:T(8,128)(2,1)S(1)} %slice.223), channel_id=1, source_target_pairs={{0,16},{1,17},{2,18},{3,19},{4,20},{5,21},{6,22},{7,23},{8,24},{9,... | collective-permute-start | bytes 393224 | tf_op jit(solution)/shard_map/ppermute | solution.py:313
  (24 other events, 44.3 us)
